TPU v7x, 32 devices: a whole 2x2x4 slice. The times are simulated.
32 devices in a mesh: row: 4 (over y, x), col: 8 (over z, core).
Axes of the slice: x: 2, y: 2, z: 4, core: 2. Of those that a mesh axis runs over, the one named last changes fastest.
Arguments:
- inputs: float32 [8, 1024, 2048], P('col', 'row'), may hold values from -6 to 6
- cotangent: float32 [8, 1024, 2048], P('col', 'row'), may hold values from -6 to 6
- image_starts: int32 [8, 2], P('col'), may hold values from 0 to 768, as said below
- owners: int32 [16], replicated, may hold values from 0 to 7, as said below
- query_master: float32 [4096, 3, 2048], P('col', None, 'row'), may hold values from -0.125 to 0.125
- query_first: float32 [4096, 3, 2048], P('col', None, 'row')
- query_second: float32 [4096, 3, 2048], P('col', None, 'row'), may hold values from 8192 to 32768
- output_master: float32 [4096, 2048], P('col', 'row'), may hold values from -1 to 1
- output_first: float32 [4096, 2048], P('col', 'row')
- output_second: float32 [4096, 2048], P('col', 'row'), may hold values from 128 to 512
- gate_master: float32 [4096, 2, 5632], P('col', None, 'row'), may hold values from -0.125 to 0.125
- gate_first: float32 [4096, 2, 5632], P('col', None, 'row')
- gate_second: float32 [4096, 2, 5632], P('col', None, 'row'), may hold values from 1024 to 4096
- down_master: float32 [4096, 5632], P('col', 'row'), may hold values from -0.078125 to 0.078125
- down_first: float32 [4096, 5632], P('col', 'row')
- down_second: float32 [4096, 5632], P('col', 'row'), may hold values from 2048 to 8192
- vector_master: float32 [4096, 7], P('col'), may hold values from -0.5 to 1.4
- vector_first: float32 [4096, 7], P('col')
- vector_second: float32 [4096, 7], P('col'), may hold values from 8192 to 32768
Outputs:
- layer_out: float32 [8, 1024, 2048], P('col', 'row')
- input_grad: float32 [8, 1024, 2048], P('col', 'row')
- query_master_new: float32 [4096, 3, 2048], P('col', None, 'row')
- query_first_new: float32 [4096, 3, 2048], P('col', None, 'row')
- query_second_new: float32 [4096, 3, 2048], P('col', None, 'row')
- output_master_new: float32 [4096, 2048], P('col', 'row')
- output_first_new: float32 [4096, 2048], P('col', 'row')
- output_second_new: float32 [4096, 2048], P('col', 'row')
- gate_master_new: float32 [4096, 2, 5632], P('col', None, 'row')
- gate_first_new: float32 [4096, 2, 5632], P('col', None, 'row')
- gate_second_new: float32 [4096, 2, 5632], P('col', None, 'row')
- down_master_new: float32 [4096, 5632], P('col', 'row')
- down_first_new: float32 [4096, 5632], P('col', 'row')
- down_second_new: float32 [4096, 5632], P('col', 'row')
- vector_master_new: float32 [4096, 7], P('col')
- vector_first_new: float32 [4096, 7], P('col')
- vector_second_new: float32 [4096, 7], P('col')
Inputs may be any that keep to these rules, and one draw needn't show every extreme that they name: `image_starts`: in each sequence the 2 image blocks of 256 positions do not intersect; block k lies within positions k * 512 to (k + 1) * 512 - 1. `owners`: each index of col owns 1 to 4 blocks, and one owns exactly 4.
All inputs are finite; a program needn't handle non-finite values.
Results may differ from a plain program's by a relative error of at most 0.023.
Values may be sent and summed in bfloat16 or wider, within the bound.
No kernel may reach another device: no remote copies, remote signals or barrier semaphores. Data moves between devices by JAX's collectives and lax.ppermute only.
A program may use at most 256 MiB of HBM per device.

v0:
```python
import math

import jax
import jax.numpy as jnp
import numpy as np
from jax import lax
from jax.experimental import pallas as pl
from jax.experimental.layout import Layout, with_layout_constraint
from jax.experimental.pallas import tpu as pltpu
from jax.sharding import PartitionSpec as P

D = 2048
HEAD_DIM = 64
FF = 5632
ROT = 16
SEQ = 1024
IMG = 256
STEP = 5
CAP = 4

LANES = 128
MIB = 1 << 20

NORM_EPSILON = 1e-05
ADAM_EPSILON = 1e-08
MOMENT_DECAY = 0.5
WEIGHT_DECAY = 0.1
ROTARY_BASE = 10000.0
MASKED_SCORE = -1e30


def owner_slots(owners):
    block_count = owners.shape[0]
    block_order = jnp.arange(block_count, dtype=jnp.int32)
    before = (owners[:, None] == owners[None, :]) & (block_order[None, :] < block_order[:, None])
    return owners * CAP + jnp.sum(before.astype(jnp.int32), axis=1)


def slot_sources(slot_of, slot_count):
    matches = slot_of[None, :] == jnp.arange(slot_count, dtype=jnp.int32)[:, None]
    filled = jnp.any(matches, axis=1)
    numbers = jnp.arange(slot_of.shape[0], dtype=jnp.int32)
    source = jnp.sum(jnp.where(matches, numbers[None, :], 0), axis=1)
    return (source, filled)


def unpack(gathered, slot_of, block_rows):
    shaped = gathered.reshape((-1, block_rows) + gathered.shape[1:])
    return jnp.take(shaped, slot_of, axis=0).reshape((-1,) + gathered.shape[1:])


def own_blocks(gradient, own_source, block_rows):
    shaped = gradient.reshape((-1, block_rows) + gradient.shape[1:])
    return jnp.take(shaped, own_source, axis=0).reshape((-1,) + gradient.shape[1:])


def normalize(values):
    center = jnp.mean(values, axis=-1, keepdims=True)
    spread = jnp.mean(values * values, axis=-1, keepdims=True) - center * center
    inverse = lax.rsqrt(spread + NORM_EPSILON)
    return ((values - center) * inverse, inverse)


def norm_back(upstream, plain_rows, inverse, gain_row):
    scaled = upstream * gain_row
    return inverse * (
        scaled
        - jnp.mean(scaled, axis=-1, keepdims=True)
        - plain_rows * jnp.mean(scaled * plain_rows, axis=-1, keepdims=True)
    )


def rotary_tables(seq_len):
    half_rot = ROT // 2
    frequency = ROTARY_BASE ** (-2.0 * jnp.arange(half_rot, dtype=jnp.float32) / ROT)
    angles = jnp.arange(seq_len, dtype=jnp.float32)[:, None] * frequency[None, :]
    return (jnp.cos(angles), jnp.sin(angles))


def rotate(values, cosine_table, sine_table):
    half_rot = ROT // 2
    first_half = values[..., :half_rot]
    second_half = values[..., half_rot:ROT]
    cosine_part = cosine_table[:, None, :]
    sine_part = sine_table[:, None, :]
    return jnp.concatenate(
        [
            first_half * cosine_part - second_half * sine_part,
            second_half * cosine_part + first_half * sine_part,
            values[..., ROT:],
        ],
        axis=-1,
    )


def rotate_back(values, cosine_table, sine_table):
    half_rot = ROT // 2
    first_half = values[..., :half_rot]
    second_half = values[..., half_rot:ROT]
    cosine_part = cosine_table[:, None, :]
    sine_part = sine_table[:, None, :]
    return jnp.concatenate(
        [
            first_half * cosine_part + second_half * sine_part,
            second_half * cosine_part - first_half * sine_part,
            values[..., ROT:],
        ],
        axis=-1,
    )


def block_ids(starts, seq_len):
    positions = jnp.arange(seq_len, dtype=jnp.int32)
    inside = (positions[None, :] >= starts[:, None]) & (positions[None, :] < starts[:, None] + IMG)
    numbers = jnp.arange(1, starts.shape[0] + 1, dtype=jnp.int32)
    return jnp.sum(jnp.where(inside, numbers[:, None], 0), axis=0)


def adam_step(master, first_state, second_state, gradient, keep_rows, rate):
    new_first = MOMENT_DECAY * first_state + (1.0 - MOMENT_DECAY) * gradient
    new_second = MOMENT_DECAY * second_state + (1.0 - MOMENT_DECAY) * gradient * gradient
    correction = 1.0 - MOMENT_DECAY**STEP
    direction = new_first / correction / (jnp.sqrt(new_second / correction) + ADAM_EPSILON)
    new_master = master - rate * (direction + WEIGHT_DECAY * master)
    keep_mask = keep_rows.reshape(keep_rows.shape + (1,) * (master.ndim - 1))
    return (
        jnp.where(keep_mask, new_master, master),
        jnp.where(keep_mask, new_first, first_state),
        jnp.where(keep_mask, new_second, second_state),
    )


def step_rates():
    return (
        2.0 / math.sqrt(D),
        2.0 / math.sqrt(D * 16 // SEQ),
        2.0 / math.sqrt(D),
        2.0 / math.sqrt(FF),
        0.5,
    )


def local(
    inputs,
    cotangent,
    image_starts,
    owners,
    query_master,
    query_first,
    query_second,
    output_master,
    output_first,
    output_second,
    gate_master,
    gate_first,
    gate_second,
    down_master,
    down_first,
    down_second,
    vector_master,
    vector_first,
    vector_second,
):
    columns = lax.axis_size("col")
    col_index = lax.axis_index("col")
    row_index = lax.axis_index("row")
    block_rows = D // owners.shape[0]
    slot_of = owner_slots(owners)
    source, filled = slot_sources(slot_of, CAP * columns)
    shared = (
        lax.all_gather(query_master.astype(jnp.bfloat16), "col", axis=0, tiled=True),
        lax.all_gather(output_master.astype(jnp.bfloat16), "col", axis=0, tiled=True),
        lax.all_gather(gate_master.astype(jnp.bfloat16), "col", axis=0, tiled=True),
        lax.all_gather(down_master.astype(jnp.bfloat16), "col", axis=0, tiled=True),
        lax.all_gather(vector_master.astype(jnp.bfloat16), "col", axis=0, tiled=True),
    )
    w_query = unpack(shared[0], slot_of, block_rows)
    w_output = unpack(shared[1], slot_of, block_rows)
    w_gate = unpack(shared[2], slot_of, block_rows)
    w_down = unpack(shared[3], slot_of, block_rows)
    vectors = unpack(shared[4], slot_of, block_rows).astype(jnp.float32)
    local_in = inputs[0]
    width = local_in.shape[1]
    head_cols = w_query.shape[2]
    local_heads = head_cols // HEAD_DIM
    score_scale = 1.0 / math.sqrt(HEAD_DIM)
    qkv_bias = lax.dynamic_slice_in_dim(vectors[:, 4:7], row_index * head_cols, head_cols, 0).T
    plain_one, inverse_one = normalize(local_in)
    normed_one = (plain_one * vectors[:, 0] + vectors[:, 1]).astype(jnp.bfloat16)
    rows_one = lax.all_gather(normed_one, "row", axis=0, tiled=True)
    seq_len = rows_one.shape[0]
    mixed_proj = (
        jnp.einsum("td,djh->tjh", rows_one, w_query, preferred_element_type=jnp.float32)
        + qkv_bias[None]
    )
    cosine_table, sine_table = rotary_tables(seq_len)
    queries = rotate(
        mixed_proj[:, 0].reshape(seq_len, local_heads, HEAD_DIM), cosine_table, sine_table
    ).astype(jnp.bfloat16)
    key_rows = rotate(
        mixed_proj[:, 1].reshape(seq_len, local_heads, HEAD_DIM), cosine_table, sine_table
    ).astype(jnp.bfloat16)
    value_rows = mixed_proj[:, 2].reshape(seq_len, local_heads, HEAD_DIM).astype(jnp.bfloat16)
    labels = block_ids(image_starts[0], seq_len)
    block_size = min(512, seq_len)
    block_count = seq_len // block_size
    positions = jnp.arange(seq_len, dtype=jnp.int32)

    def scores_at(first_row):
        row_pos = first_row + jnp.arange(block_size, dtype=jnp.int32)
        row_label = lax.dynamic_slice_in_dim(labels, first_row, block_size, 0)
        allowed = (positions[None, :] <= row_pos[:, None]) | (
            row_label[:, None] == labels[None, :]
        ) & (row_label[:, None] > 0)
        query_rows = lax.dynamic_slice_in_dim(queries, first_row, block_size, 0)
        raw_scores = (
            jnp.einsum("qhe,khe->hqk", query_rows, key_rows, preferred_element_type=jnp.float32)
            * score_scale
        )
        return (jnp.where(allowed[None], raw_scores, MASKED_SCORE), query_rows)

    def forward_block(block_index):
        scores, query_rows = scores_at(block_index * block_size)
        row_peak = jnp.max(scores, axis=-1, keepdims=True)
        powers = jnp.exp(scores - row_peak)
        row_total = jnp.sum(powers, axis=-1, keepdims=True)
        weights = (powers / row_total).astype(jnp.bfloat16)
        output = jnp.einsum("hqk,khe->qhe", weights, value_rows, preferred_element_type=jnp.float32)
        return (output, (row_peak + jnp.log(row_total))[..., 0])

    output_blocks, log_totals = lax.map(forward_block, jnp.arange(block_count, dtype=jnp.int32))
    attended = output_blocks.reshape(seq_len, head_cols).astype(jnp.bfloat16)
    picked_rows = attended
    middle = local_in + lax.psum_scatter(
        jnp.einsum("th,dh->td", picked_rows, w_output, preferred_element_type=jnp.float32),
        "row",
        scatter_dimension=0,
        tiled=True,
    )
    plain_two, inverse_two = normalize(middle)
    normed_two = (plain_two * vectors[:, 2] + vectors[:, 3]).astype(jnp.bfloat16)
    rows_two = lax.all_gather(normed_two, "row", axis=0, tiled=True)
    gate_up = jnp.einsum("td,djf->tjf", rows_two, w_gate, preferred_element_type=jnp.float32)
    gate_part = gate_up[:, 0]
    up_part = gate_up[:, 1]
    gate_sigmoid = jax.nn.sigmoid(gate_part)
    activated = gate_part * gate_sigmoid
    hidden = (activated * up_part).astype(jnp.bfloat16)
    picked_rows = hidden
    layer_out = middle + lax.psum_scatter(
        jnp.einsum("tf,df->td", picked_rows, w_down, preferred_element_type=jnp.float32).astype(
            jnp.bfloat16
        ),
        "row",
        scatter_dimension=0,
        tiled=True,
    ).astype(jnp.float32)
    upstream = cotangent[0]
    rows_grad = lax.all_gather(upstream.astype(jnp.bfloat16), "row", axis=0, tiled=True)
    hidden_grad = jnp.einsum("td,df->tf", rows_grad, w_down, preferred_element_type=jnp.float32)
    down_grad = jnp.einsum("tf,td->df", hidden, rows_grad, preferred_element_type=jnp.float32)
    gate_grad = hidden_grad * up_part * gate_sigmoid * (1.0 + gate_part * (1.0 - gate_sigmoid))
    up_grad = hidden_grad * activated
    gate_up_grad = jnp.stack([gate_grad, up_grad], axis=1).astype(jnp.bfloat16)
    gate_weight_grad = jnp.einsum(
        "td,tjf->djf", rows_two, gate_up_grad, preferred_element_type=jnp.float32
    )
    picked_rows = gate_up_grad
    normed_two_grad = lax.psum_scatter(
        jnp.einsum("tjf,djf->td", picked_rows, w_gate, preferred_element_type=jnp.float32),
        "row",
        scatter_dimension=0,
        tiled=True,
    )
    middle_grad = upstream + norm_back(normed_two_grad, plain_two, inverse_two, vectors[:, 2])
    rows_mid = lax.all_gather(middle_grad.astype(jnp.bfloat16), "row", axis=0, tiled=True)
    attended_grad = jnp.einsum(
        "td,dh->th", rows_mid, w_output, preferred_element_type=jnp.float32
    ).astype(jnp.bfloat16)
    output_grad = jnp.einsum("th,td->dh", attended, rows_mid, preferred_element_type=jnp.float32)
    head_grad = attended_grad.reshape(seq_len, local_heads, HEAD_DIM)

    def backward_block(running, block_index):
        key_total, value_total = running
        first_row = block_index * block_size
        scores, query_rows = scores_at(first_row)
        probabilities = jnp.exp(scores - log_totals[block_index][..., None])
        row_grad = lax.dynamic_slice_in_dim(head_grad, first_row, block_size, 0)
        prob_grad = jnp.einsum(
            "qhe,khe->hqk", row_grad, value_rows, preferred_element_type=jnp.float32
        )
        inner = jnp.sum(prob_grad * probabilities, axis=-1, keepdims=True)
        score_grad = (probabilities * (prob_grad - inner)).astype(jnp.bfloat16)
        query_grad = (
            jnp.einsum("hqk,khe->qhe", score_grad, key_rows, preferred_element_type=jnp.float32)
            * score_scale
        )
        key_total = (
            key_total
            + jnp.einsum("hqk,qhe->khe", score_grad, query_rows, preferred_element_type=jnp.float32)
            * score_scale
        )
        value_total = value_total + jnp.einsum(
            "hqk,qhe->khe",
            probabilities.astype(jnp.bfloat16),
            row_grad,
            preferred_element_type=jnp.float32,
        )
        return ((key_total, value_total), query_grad)

    empty_heads = jnp.zeros((seq_len, local_heads, HEAD_DIM), jnp.float32)
    (key_grad, value_grad), query_blocks = lax.scan(
        backward_block, (empty_heads, empty_heads), jnp.arange(block_count, dtype=jnp.int32)
    )
    query_grad = query_blocks.reshape(seq_len, local_heads, HEAD_DIM)
    mixed_grad = jnp.stack(
        [
            rotate_back(query_grad, cosine_table, sine_table).reshape(seq_len, head_cols),
            rotate_back(key_grad, cosine_table, sine_table).reshape(seq_len, head_cols),
            value_grad.reshape(seq_len, head_cols),
        ],
        axis=1,
    ).astype(jnp.bfloat16)
    bias_grad = jnp.sum(mixed_grad, axis=0, dtype=jnp.float32)
    query_weight_grad = jnp.einsum(
        "td,tjh->djh", rows_one, mixed_grad, preferred_element_type=jnp.float32
    )
    picked_rows = mixed_grad
    normed_one_grad = lax.psum_scatter(
        jnp.einsum("tjh,djh->td", picked_rows, w_query, preferred_element_type=jnp.float32).astype(
            jnp.bfloat16
        ),
        "row",
        scatter_dimension=0,
        tiled=True,
    ).astype(jnp.float32)
    input_grad = middle_grad + norm_back(normed_one_grad, plain_one, inverse_one, vectors[:, 0])
    norm_grads = jnp.stack(
        [
            jnp.sum(normed_one_grad * plain_one, axis=0),
            jnp.sum(normed_one_grad, axis=0),
            jnp.sum(normed_two_grad * plain_two, axis=0),
            jnp.sum(normed_two_grad, axis=0),
        ],
        axis=1,
    )
    placed = lax.dynamic_update_slice_in_dim(
        jnp.zeros((width, 3), jnp.float32), bias_grad.T, row_index * head_cols, 0
    )
    vector_grad = lax.psum(
        jnp.concatenate([norm_grads, placed], axis=1).astype(jnp.bfloat16), "row"
    )
    own_filled = lax.dynamic_slice_in_dim(filled, col_index * CAP, CAP, 0)
    own_source = lax.dynamic_slice_in_dim(source, col_index * CAP, CAP, 0)
    summed = (
        lax.psum(query_weight_grad.astype(jnp.bfloat16), "col").astype(jnp.float32),
        lax.psum(output_grad.astype(jnp.bfloat16), "col").astype(jnp.float32),
        lax.psum(gate_weight_grad.astype(jnp.bfloat16), "col").astype(jnp.float32),
        lax.psum(down_grad.astype(jnp.bfloat16), "col").astype(jnp.float32),
        lax.psum(vector_grad, "col").astype(jnp.float32),
    )
    owned_grads = tuple((own_blocks(whole_grad, own_source, block_rows) for whole_grad in summed))
    keep_rows = jnp.repeat(own_filled, block_rows)
    masters = (query_master, output_master, gate_master, down_master, vector_master)
    firsts = (query_first, output_first, gate_first, down_first, vector_first)
    seconds = (query_second, output_second, gate_second, down_second, vector_second)
    rates = step_rates()
    updated = [
        adam_step(
            masters[kind_index],
            firsts[kind_index],
            seconds[kind_index],
            owned_grads[kind_index],
            keep_rows,
            rates[kind_index],
        )
        for kind_index in range(5)
    ]
    return (
        layer_out[None],
        input_grad[None],
        updated[0][0],
        updated[0][1],
        updated[0][2],
        updated[1][0],
        updated[1][1],
        updated[1][2],
        updated[2][0],
        updated[2][1],
        updated[2][2],
        updated[3][0],
        updated[3][1],
        updated[3][2],
        updated[4][0],
        updated[4][1],
        updated[4][2],
    )


BF16 = jnp.bfloat16
F32 = jnp.float32


def smem():
    return pl.BlockSpec(memory_space=pltpu.SMEM)


def params(mib=16):
    return pltpu.CompilerParams(vmem_limit_bytes=mib * MIB)


def cost(flops, nbytes, powers=0):
    return pl.CostEstimate(flops=int(flops), bytes_accessed=int(nbytes), transcendentals=int(powers))


def lane_block(number):
    return pl.ds(pl.multiple_of(number * LANES, LANES), LANES)


def after(value, *others):
    return lax.optimization_barrier((value, *others))[0]


LIVE, PLACES, UNEVEN, TABLE = 10, 14, 18, 32


def plan_blocks(owners, places, columns, head_blocks):
    blocks = owners.shape[0]
    half = blocks // (columns // 2)

    def kernel(owner_ref, at_ref, table_ref, order_ref, sorted_ref, head_slot_ref, head_ref):
        held = [owner_ref[block] for block in range(blocks)]
        col, row = at_ref[0], at_ref[1]
        chip = lax.shift_right_logical(col, 1)
        core = jnp.bitwise_and(col, 1)

        def total(flags):
            return sum(flag.astype(jnp.int32) for flag in flags)

        def below(index):
            return total(owner < index for owner in held)

        for block in range(blocks):
            rank = total(held[other] == held[block] for other in range(block)) + jnp.int32(0)
            place = below(held[block]) + rank
            slot = held[block] * CAP + rank
            order_ref[place] = jnp.int32(block)
            sorted_ref[place] = slot
            head = block - row * head_blocks

            @pl.when((head >= 0) & (head < head_blocks))
            def mine(head=head, slot=slot, place=place):
                head_slot_ref[head] = slot
                head_ref[head] = place

        first = below(2 * chip)
        middle = below(2 * chip + 1)
        end = below(2 * chip + 2)
        own_first = below(col)
        own_count = below(col + 1) - own_first

        def chip_code(place):
            second = place >= middle
            rank = place - jnp.where(second, middle, first)
            code = jnp.where(second.astype(jnp.int32) == core, 0, 16) + rank
            return jnp.where((place >= first) & (place < end), code, 0)

        toward = 1 - 2 * core
        for index in range(2):
            offset = 2 * core + index
            table_ref[index] = chip_code(half * (chip + toward) + offset)
            table_ref[2 + index] = chip_code(half * (chip - toward) + offset)
            kept = half * chip + offset
            near, far = 32 + index, 48 + index
            table_ref[4 + index] = jnp.where(
                kept < first,
                jnp.where(core == 0, near, far),
                jnp.where(kept >= end, jnp.where(core == 0, far, near), chip_code(kept)),
            )
        for rank in range(CAP):
            live = rank < own_count
            place = own_first + jnp.minimum(rank, own_count - 1)
            there = lax.shift_right_logical(place, 2)
            side = there - chip
            other = lax.shift_right_logical(place - half * there, 1)
            near_side = 1 - 2 * other
            same = other == core
            source = jnp.where(
                side == 0,
                jnp.where(same, 0, 2),
                jnp.where(side == near_side, jnp.where(same, 1, 3), jnp.where(same, 4, 5)),
            )
            table_ref[6 + rank] = 16 * source + jnp.bitwise_and(place, 1)
            table_ref[LIVE + rank] = live.astype(jnp.int32)
            table_ref[PLACES + rank] = place
        widest = jnp.int32(0)
        for number in range(1, columns // 2):
            widest = jnp.maximum(widest, jnp.abs(below(2 * number) - half * number))
        table_ref[UNEVEN] = jnp.clip(widest - 2, 0, 2)
        table_ref[UNEVEN + 1] = chip_code(half * (chip - toward) + 1 + core)
        for index in range(UNEVEN + 2, TABLE):
            table_ref[index] = jnp.int32(0)

    def ints(size):
        return jax.ShapeDtypeStruct((size,), jnp.int32)

    return pl.pallas_call(
        kernel,
        in_specs=[smem(), smem()],
        out_specs=[smem()] * 5,
        out_shape=[ints(TABLE), ints(blocks), ints(blocks), ints(head_blocks), ints(head_blocks)],
        compiler_params=params(),
        name="plan_blocks",
    )(owners, places)


def pack_attention(slabs, output):
    kinds, rows, width = slabs.shape
    block = rows // CAP
    total = kinds * width + output.shape[1]

    def kernel(in_ref, output_ref, out_ref):
        for kind in range(kinds):
            out_ref[0, :, kind * width : (kind + 1) * width] = in_ref[kind].astype(BF16)
        out_ref[0, :, kinds * width :] = output_ref[...].astype(BF16)

    return pl.pallas_call(
        kernel,
        grid=(CAP,),
        in_specs=[
            pl.BlockSpec((kinds, block, width), lambda s: (0, s, 0)),
            pl.BlockSpec((block, output.shape[1]), lambda s: (s, 0)),
        ],
        out_specs=pl.BlockSpec((1, block, total), lambda s: (s, 0, 0)),
        out_shape=jax.ShapeDtypeStruct((CAP, block, total), BF16),
        compiler_params=params(58),
        cost_estimate=cost(0, 6 * rows * total),
        name="pack_attention",
    )(slabs, output)


def after(value, *others):
    return lax.optimization_barrier((value, *others))[0]


def gate_lines(values):
    rows, kinds, width = values.shape
    split = with_layout_constraint(
        values.reshape(rows, kinds, width // LANES, LANES), Layout(major_to_minor=(0, 2, 1, 3))
    )
    return jnp.transpose(split, (0, 2, 1, 3)).reshape(rows * kinds * width // LANES, LANES)


def gate_unlines(lines, shape):
    rows, kinds, width = shape
    split = jnp.transpose(lines.reshape(rows, width // LANES, kinds, LANES), (0, 2, 1, 3))
    return with_layout_constraint(split, Layout(major_to_minor=(0, 2, 1, 3))).reshape(shape)


def pack_flat(name, master):
    rows, width = master.shape
    block = rows // CAP

    def kernel(in_ref, out_ref):
        out_ref[0] = in_ref[...].astype(BF16)

    return pl.pallas_call(
        kernel,
        grid=(CAP,),
        in_specs=[pl.BlockSpec((block, width), lambda s: (s, 0))],
        out_specs=pl.BlockSpec((1, block, width), lambda s: (s, 0, 0)),
        out_shape=jax.ShapeDtypeStruct((CAP, block, width), BF16),
        compiler_params=params(),
        cost_estimate=cost(0, 6 * rows * width),
        name=name,
    )(master)


def pack_gate(lines, rows):
    block = rows // CAP
    tiles = lines.shape[0] // rows

    def kernel(in_ref, out_ref):
        for tile in range(tiles):
            out_ref[0, :, tile * LANES : (tile + 1) * LANES] = in_ref[
                pl.ds(tile, block, stride=tiles), :
            ].astype(BF16)

    return pl.pallas_call(
        kernel,
        grid=(CAP,),
        in_specs=[pl.BlockSpec((block * tiles, LANES), lambda s: (s, 0))],
        out_specs=pl.BlockSpec((1, block, tiles * LANES), lambda s: (s, 0, 0)),
        out_shape=jax.ShapeDtypeStruct((CAP, block, tiles * LANES), BF16),
        compiler_params=params(58),
        cost_estimate=cost(0, 6 * lines.size),
        name="pack_gate",
    )(lines)


def pick_blocks(codes, first, count, sources):
    shape = sources[0].shape[1:]

    def kernel(code_ref, *refs):
        ins, out, sems = refs[: len(sources)], refs[-2], refs[-1]
        for place in range(count):
            code = code_ref[first + place]
            index = jnp.bitwise_and(code, 15)
            origin = lax.shift_right_logical(code, 4)
            for number, source in enumerate(ins):

                @pl.when(origin == number)
                def start(source=source, index=index, place=place):
                    held = source.at[index if source.shape[0] > 1 else 0]
                    pltpu.make_async_copy(held, out.at[place], sems.at[place]).start()

        for place in range(count):
            pltpu.make_async_copy(ins[0].at[0], out.at[place], sems.at[place]).wait()

    moved = count * shape[0] * shape[1]
    return pl.pallas_call(
        kernel,
        in_specs=[smem()] + [pl.BlockSpec(memory_space=pl.ANY)] * len(sources),
        out_specs=pl.BlockSpec(memory_space=pltpu.VMEM),
        out_shape=jax.ShapeDtypeStruct((count, *shape), BF16),
        scratch_shapes=[pltpu.SemaphoreType.DMA((count,))],
        compiler_params=params(),
        cost_estimate=cost(0, 4 * moved),
        name="pick_blocks",
    )(codes, *sources)


def row_blocks(height, width, first=0):
    return pl.BlockSpec((height, width), lambda i: (i + first, 0))


def whole(height, width):
    return pl.BlockSpec((height, width), lambda i: (0, 0))


NORM_ROWS = 64


def statistics(values):
    center = jnp.mean(values, axis=-1, keepdims=True)
    spread = jnp.mean(values * values, axis=-1, keepdims=True) - center * center
    return center, lax.rsqrt(spread + NORM_EPSILON)


def order_grad(order, cotangent):
    rows, width = cotangent.shape

    def kernel(order_ref, in_ref, out_ref):
        for place in range(width // LANES):
            out_ref[:, place * LANES : (place + 1) * LANES] = in_ref[
                :, lane_block(order_ref[place])
            ].astype(BF16)

    return pl.pallas_call(
        kernel,
        grid=(rows // NORM_ROWS,),
        in_specs=[smem(), row_blocks(NORM_ROWS, width)],
        out_specs=row_blocks(NORM_ROWS, width),
        out_shape=jax.ShapeDtypeStruct((rows, width), BF16),
        compiler_params=params(),
        cost_estimate=cost(0, 6 * rows * width),
        name="order_grad",
    )(order, cotangent)


def norm_one(order, inputs):
    rows, width = inputs.shape

    def kernel(order_ref, in_ref, out_ref):
        center, inverse = statistics(in_ref[...])
        for place in range(width // LANES):
            span = slice(place * LANES, (place + 1) * LANES)
            plain = (in_ref[:, lane_block(order_ref[place])] - center) * inverse
            out_ref[:, span] = plain.astype(BF16)

    return pl.pallas_call(
        kernel,
        grid=(rows // NORM_ROWS,),
        in_specs=[smem(), row_blocks(NORM_ROWS, width)],
        out_specs=row_blocks(NORM_ROWS, width),
        out_shape=jax.ShapeDtypeStruct((rows, width), BF16),
        compiler_params=params(),
        cost_estimate=cost(0, 6 * rows * width),
        name="norm_one",
    )(order, inputs)


def scale_rows(plain, vectors):
    rows, width = plain.shape
    tile = 256

    def kernel(in_ref, vec_ref, out_ref):
        out_ref[...] = (in_ref[...].astype(F32) * vec_ref[0:1, :] + vec_ref[1:2, :]).astype(BF16)

    return pl.pallas_call(
        kernel,
        grid=(rows // tile,),
        in_specs=[row_blocks(tile, width), whole(8, width)],
        out_specs=row_blocks(tile, width),
        out_shape=jax.ShapeDtypeStruct((rows, width), BF16),
        compiler_params=params(),
        cost_estimate=cost(0, 4 * rows * width),
        name="scale_rows",
    )(plain, vectors)


def norm_two(order, inputs, partial, vectors):
    rows, width = inputs.shape
    own, from_x, from_y = partial

    def kernel(order_ref, in_ref, own_ref, x_ref, y_ref, vec_ref, mid_ref, out_ref):
        for place in range(width // LANES):
            span = slice(place * LANES, (place + 1) * LANES)
            mid_ref[:, span] = (
                in_ref[:, lane_block(order_ref[place])]
                + own_ref[:, span].astype(F32)
                + x_ref[:, span].astype(F32)
                + y_ref[:, span].astype(F32)
            )
        middle = mid_ref[...]
        center, inverse = statistics(middle)
        plain = (middle - center) * inverse
        out_ref[...] = (plain * vec_ref[2:3, :] + vec_ref[3:4, :]).astype(BF16)

    spec = row_blocks(NORM_ROWS, width)
    return pl.pallas_call(
        kernel,
        grid=(rows // NORM_ROWS,),
        in_specs=[smem(), spec, spec, spec, spec, whole(8, width)],
        out_specs=[spec, spec],
        out_shape=[
            jax.ShapeDtypeStruct((rows, width), F32),
            jax.ShapeDtypeStruct((rows, width), BF16),
        ],
        compiler_params=params(),
        cost_estimate=cost(0, 16 * rows * width),
        name="norm_two",
    )(order, inputs, own, from_x, from_y, vectors)


def finish_out(order, middle, partial):
    rows, width = middle.shape
    own, from_x, from_y = partial

    def kernel(order_ref, mid_ref, own_ref, x_ref, y_ref, out_ref):
        for place in range(width // LANES):
            span = slice(place * LANES, (place + 1) * LANES)
            out_ref[:, lane_block(order_ref[place])] = (
                mid_ref[:, span]
                + own_ref[:, span].astype(F32)
                + x_ref[:, span].astype(F32)
                + y_ref[:, span].astype(F32)
            )

    spec = row_blocks(NORM_ROWS, width)
    return pl.pallas_call(
        kernel,
        grid=(rows // NORM_ROWS,),
        in_specs=[smem(), spec, spec, spec, spec],
        out_specs=spec,
        out_shape=jax.ShapeDtypeStruct((rows, width), F32),
        compiler_params=params(),
        cost_estimate=cost(0, 14 * rows * width),
        name="finish_out",
    )(order, middle, own, from_x, from_y)


def norm_pull(upstream, plain, inverse, gain):
    scaled = upstream * gain
    return inverse * (
        scaled
        - jnp.mean(scaled, axis=-1, keepdims=True)
        - plain * jnp.mean(scaled * plain, axis=-1, keepdims=True)
    )


def add_sums(sum_ref, upstream, plain):
    @pl.when(pl.program_id(0) == 0)
    def clear():
        sum_ref[...] = jnp.zeros_like(sum_ref)

    sum_ref[0:1, :] += jnp.sum(upstream * plain, axis=0, keepdims=True)
    sum_ref[1:2, :] += jnp.sum(upstream, axis=0, keepdims=True)


def norm_two_back(order, cotangent, middle, partial, vectors):
    rows, width = middle.shape
    own, from_x, from_y = partial

    def kernel(
        order_ref, cot_ref, mid_ref, own_ref, x_ref, y_ref, vec_ref, grad_ref, low_ref, sum_ref
    ):
        middle_rows = mid_ref[...]
        center, inverse = statistics(middle_rows)
        plain = (middle_rows - center) * inverse
        upstream = own_ref[...].astype(F32) + x_ref[...].astype(F32) + y_ref[...].astype(F32)
        add_sums(sum_ref, upstream, plain)
        grad_ref[...] = norm_pull(upstream, plain, inverse, vec_ref[2:3, :])
        for place in range(width // LANES):
            span = slice(place * LANES, (place + 1) * LANES)
            total = grad_ref[:, span] + cot_ref[:, lane_block(order_ref[place])]
            grad_ref[:, span] = total
            low_ref[:, span] = total.astype(BF16)

    spec = row_blocks(NORM_ROWS, width)
    return pl.pallas_call(
        kernel,
        grid=(rows // NORM_ROWS,),
        in_specs=[smem(), spec, spec, spec, spec, spec, whole(8, width)],
        out_specs=[spec, spec, whole(8, width)],
        out_shape=[
            jax.ShapeDtypeStruct((rows, width), F32),
            jax.ShapeDtypeStruct((rows, width), BF16),
            jax.ShapeDtypeStruct((8, width), F32),
        ],
        compiler_params=params(),
        cost_estimate=cost(0, 20 * rows * width),
        name="norm_two_back",
    )(order, cotangent, middle, own, from_x, from_y, vectors)


def norm_one_back(order, inputs, middle_grad, partial, vectors):
    rows, width = inputs.shape
    own, from_x, from_y = partial

    def kernel(
        order_ref,
        in_ref,
        mid_ref,
        own_ref,
        x_ref,
        y_ref,
        vec_ref,
        out_ref,
        sum_ref,
        plain_ref,
        pull_ref,
    ):
        center, inverse = statistics(in_ref[...])
        for place in range(width // LANES):
            span = slice(place * LANES, (place + 1) * LANES)
            plain_ref[:, span] = (in_ref[:, lane_block(order_ref[place])] - center) * inverse
        plain = plain_ref[...]
        upstream = own_ref[...].astype(F32) + x_ref[...].astype(F32) + y_ref[...].astype(F32)
        add_sums(sum_ref, upstream, plain)
        pull_ref[...] = norm_pull(upstream, plain, inverse, vec_ref[0:1, :])
        for place in range(width // LANES):
            span = slice(place * LANES, (place + 1) * LANES)
            out_ref[:, lane_block(order_ref[place])] = mid_ref[:, span] + pull_ref[:, span]

    spec = row_blocks(NORM_ROWS, width)
    return pl.pallas_call(
        kernel,
        grid=(rows // NORM_ROWS,),
        in_specs=[smem(), spec, spec, spec, spec, spec, whole(8, width)],
        out_specs=[spec, whole(8, width)],
        out_shape=[
            jax.ShapeDtypeStruct((rows, width), F32),
            jax.ShapeDtypeStruct((8, width), F32),
        ],
        scratch_shapes=[pltpu.VMEM((NORM_ROWS, width), F32), pltpu.VMEM((NORM_ROWS, width), F32)],
        compiler_params=params(),
        cost_estimate=cost(0, 18 * rows * width),
        name="norm_one_back",
    )(order, inputs, middle_grad, own, from_x, from_y, vectors)


def spread_vectors(sorted_slots, head_slots, gathered):
    places = sorted_slots.shape[0]
    heads = head_slots.shape[0]

    def kernel(sorted_ref, head_ref, in_ref, vec_ref, bias_ref):
        for place in range(places):
            vec_ref[:, place * LANES : (place + 1) * LANES] = in_ref[sorted_ref[place]].astype(F32)
        for place in range(heads):
            bias_ref[:, place * LANES : (place + 1) * LANES] = in_ref[head_ref[place]].astype(F32)

    return pl.pallas_call(
        kernel,
        in_specs=[smem(), smem(), pl.BlockSpec(memory_space=pltpu.VMEM)],
        out_shape=[
            jax.ShapeDtypeStruct((16, places * LANES), F32),
            jax.ShapeDtypeStruct((16, heads * LANES), F32),
        ],
        compiler_params=params(),
        name="spread_vectors",
    )(sorted_slots, head_slots, gathered)


def place_vector_grads(head_places, sums_one, sums_two, bias_sums):
    heads = head_places.shape[0]

    def kernel(head_ref, one_ref, two_ref, bias_ref, out_ref):
        out_ref[0:2, :] = one_ref[0:2, :]
        out_ref[2:4, :] = two_ref[0:2, :]
        out_ref[4:8, :] = jnp.zeros((4, out_ref.shape[1]), F32)
        for place in range(heads):
            for kind in range(3):
                first = (kind * heads + place) * LANES
                out_ref[4 + kind : 5 + kind, lane_block(head_ref[place])] = bias_ref[
                    0:1, first : first + LANES
                ]

    return pl.pallas_call(
        kernel,
        in_specs=[smem()] + [pl.BlockSpec(memory_space=pltpu.VMEM)] * 3,
        out_shape=jax.ShapeDtypeStruct(sums_one.shape, F32),
        compiler_params=params(),
        name="place_vector_grads",
    )(head_places, sums_one, sums_two, bias_sums)


def adam_vector(keep, states, gradient, rate):
    kinds, rows = states[0].shape
    block = rows // CAP

    def kernel(keep_ref, m_ref, f_ref, s_ref, g_ref, mo_ref, fo_ref, so_ref):
        for slot in range(CAP):
            span = slice(slot * block, (slot + 1) * block)
            grad = g_ref[:, lane_block(keep_ref[PLACES + slot])][:kinds]
            mo_ref[:, span], fo_ref[:, span], so_ref[:, span] = adam_update(
                m_ref[:, span], f_ref[:, span], s_ref[:, span], grad, keep_ref[LIVE + slot] > 0, rate
            )

    return pl.pallas_call(
        kernel,
        in_specs=[smem()] + [pl.BlockSpec(memory_space=pltpu.VMEM)] * 4,
        out_shape=[jax.ShapeDtypeStruct(states[0].shape, F32)] * 3,
        compiler_params=params(),
        name="adam_vector",
    )(keep, *states, gradient)


def lane_tables(seq_len):
    half = ROT // 2
    frequency = (ROTARY_BASE ** (-2.0 * np.arange(half, dtype=np.float32) / ROT)).astype(np.float32)
    angles = np.arange(seq_len, dtype=np.float32)[:, None] * frequency[None, :]
    cosine = np.cos(angles).astype(np.float32)
    sine = np.sin(angles).astype(np.float32)
    rest = HEAD_DIM - ROT
    ones = np.ones((seq_len, rest), np.float32)
    none = np.zeros((seq_len, rest), np.float32)
    blank = np.zeros((seq_len, half), np.float32)
    keep = np.concatenate([cosine, cosine, ones], axis=1)
    lower = np.concatenate([-sine, blank, none], axis=1)
    upper = np.concatenate([blank, sine, none], axis=1)
    return tuple(jnp.asarray(np.concatenate([table, table], axis=1)) for table in (keep, lower, upper))


def turn(values, keep, lower, upper):
    half = ROT // 2
    return (
        values * keep
        + pltpu.roll(values, LANES - half, 1) * lower
        + pltpu.roll(values, half, 1) * upper
    )


def head_mask(rows, head):
    lanes = lax.broadcasted_iota(jnp.int32, (rows, LANES), 1)
    return (lanes // HEAD_DIM) == head


def dot_nt(left, right):
    return lax.dot_general(left, right, (((1,), (1,)), ((), ())), preferred_element_type=F32)


def dot_nn(left, right):
    return lax.dot_general(left, right, (((1,), (0,)), ((), ())), preferred_element_type=F32)


def fill_masks(starts_ref, mask_ref, region):
    for part in range(2):
        keys = part * region + lax.broadcasted_iota(jnp.int32, (region, region), 0)
        queries = part * region + lax.broadcasted_iota(jnp.int32, (region, region), 1)
        visible = keys <= queries
        for image in range(starts_ref.shape[1]):
            first = starts_ref[0, image]
            visible = visible | (
                (keys >= first)
                & (keys < first + IMG)
                & (queries >= first)
                & (queries < first + IMG)
            )
        mask_ref[part] = jnp.where(visible, 0.0, MASKED_SCORE)


def tile_scores(key_rows, query_tile, mask_ref, part, first, tile, region):
    scores = dot_nt(key_rows, query_tile)
    mask = mask_ref[part, :, first : first + tile]
    if part == 0:
        return scores + mask
    return jnp.concatenate([scores[:region], scores[region:] + mask], axis=0)


def attend(row, starts, mixed, bias, tables):
    seq_len = mixed.shape[0]
    width = mixed.shape[1] // 3
    pairs = width // LANES
    tile = seq_len // 4
    region = seq_len // 2
    scale = 1.0 / math.sqrt(HEAD_DIM)

    def kernel(
        row_ref,
        starts_ref,
        q_ref,
        k_ref,
        v_ref,
        qb_ref,
        kb_ref,
        vb_ref,
        keep_ref,
        lower_ref,
        upper_ref,
        out_ref,
        qo_ref,
        ko_ref,
        vo_ref,
        log_ref,
        mask_ref,
    ):
        @pl.when(pl.program_id(0) == 0)
        def masks():
            fill_masks(starts_ref, mask_ref, region)

        for number in range(4):
            place = slice(number * tile, (number + 1) * tile)
            origin = pl.ds(pl.multiple_of(jnp.bitwise_xor(row_ref[0], number) * tile, tile), tile)
            turns = (keep_ref[place, :], lower_ref[place, :], upper_ref[place, :])
            turned = turn(q_ref[origin, :] + qb_ref[4:5, :], *turns)
            qo_ref[place, :] = (turned.astype(BF16).astype(F32) * scale).astype(BF16)
            ko_ref[place, :] = turn(k_ref[origin, :] + kb_ref[5:6, :], *turns).astype(BF16)
            vo_ref[place, :] = (v_ref[origin, :] + vb_ref[6:7, :]).astype(BF16)
        value_columns = jnp.transpose(vo_ref[...])
        for number in range(4):
            part = number // 2
            seen = region * (part + 1)
            first = (number % 2) * tile
            outs = []
            for head in range(2):
                query_tile = jnp.where(
                    head_mask(tile, head),
                    qo_ref[number * tile : (number + 1) * tile, :],
                    jnp.zeros((), BF16),
                )
                scores = tile_scores(
                    ko_ref[:seen, :], query_tile, mask_ref, part, first, tile, region
                )
                peak = jnp.max(scores, axis=0, keepdims=True)
                powers = jnp.exp(scores - peak)
                total = jnp.sum(powers, axis=0, keepdims=True)
                log_ref[0, head : head + 1, number * tile : (number + 1) * tile] = peak + jnp.log(
                    total
                )
                mixed_values = dot_nn(
                    value_columns[head * HEAD_DIM : (head + 1) * HEAD_DIM, :seen],
                    powers.astype(BF16),
                )
                outs.append(mixed_values / total)
            place = pl.ds(pl.multiple_of(jnp.bitwise_xor(row_ref[0], number) * tile, tile), tile)
            out_ref[place, :] = jnp.transpose(jnp.concatenate(outs, axis=0)).astype(BF16)

    def columns(kind):
        return pl.BlockSpec((seq_len, LANES), lambda h: (0, kind * pairs + h))

    bias_block = pl.BlockSpec((8, LANES), lambda h: (0, h))
    table = pl.BlockSpec((seq_len, LANES), lambda h: (0, 0))
    low = jax.ShapeDtypeStruct((seq_len, width), BF16)
    return pl.pallas_call(
        kernel,
        grid=(pairs,),
        in_specs=[smem(), smem()]
        + [columns(0), columns(1), columns(2)]
        + [bias_block] * 3
        + [table] * 3,
        out_specs=[columns(0)] * 4 + [pl.BlockSpec((1, 8, seq_len), lambda h: (h, 0, 0))],
        out_shape=[low] * 4 + [jax.ShapeDtypeStruct((pairs, 8, seq_len), F32)],
        scratch_shapes=[pltpu.VMEM((2, region, region), F32)],
        compiler_params=params(40),
        cost_estimate=cost(
            3 * seq_len * seq_len * width * 4, 20 * seq_len * width, seq_len * seq_len * 2 * pairs
        ),
        name="attend",
    )(row, starts, mixed, mixed, mixed, bias, bias, bias, *tables)


def attend_back(row, starts, queries, keys, values, logs, outputs, grads, tables):
    seq_len, width = queries.shape
    pairs = width // LANES
    tile = seq_len // 4
    region = seq_len // 2
    scale = 1.0 / math.sqrt(HEAD_DIM)

    def kernel(
        row_ref,
        starts_ref,
        q_ref,
        k_ref,
        v_ref,
        log_ref,
        o_ref,
        g_ref,
        keep_ref,
        lower_ref,
        upper_ref,
        out_ref,
        sum_ref,
        mask_ref,
        dq_ref,
        dk_ref,
        dv_ref,
        low_ref,
        bias_ref,
    ):
        @pl.when((pl.program_id(0) == 0) & (pl.program_id(1) == 0))
        def masks():
            fill_masks(starts_ref, mask_ref, region)

        @pl.when(pl.program_id(1) == 0)
        def work():
            dk_ref[...] = jnp.zeros_like(dk_ref)
            dv_ref[...] = jnp.zeros_like(dv_ref)
            key_columns = jnp.transpose(k_ref[...])
            for number in range(4):
                part = number // 2
                seen = region * (part + 1)
                first = (number % 2) * tile
                span = slice(number * tile, (number + 1) * tile)
                origin = pl.ds(
                    pl.multiple_of(jnp.bitwise_xor(row_ref[0], number) * tile, tile), tile
                )
                grad_tile = g_ref[origin, :]
                products = jnp.transpose(grad_tile.astype(F32) * o_ref[origin, :].astype(F32))
                query_grads = []
                for head in range(2):
                    mine = head_mask(tile, head)
                    query_tile = jnp.where(mine, q_ref[span, :], jnp.zeros((), BF16))
                    head_grad = jnp.where(mine, grad_tile, jnp.zeros((), BF16))
                    inner = jnp.sum(
                        products[head * HEAD_DIM : (head + 1) * HEAD_DIM], axis=0, keepdims=True
                    )
                    scores = tile_scores(
                        k_ref[:seen, :], query_tile, mask_ref, part, first, tile, region
                    )
                    weights = jnp.exp(scores - log_ref[0, head : head + 1, span])
                    pulls = dot_nt(v_ref[:seen, :], head_grad)
                    score_grad = (weights * (pulls - inner)).astype(BF16)
                    dv_ref[:seen, :] += dot_nn(weights.astype(BF16), head_grad)
                    dk_ref[:seen, :] += dot_nn(score_grad, query_tile)
                    query_grads.append(
                        dot_nn(
                            key_columns[head * HEAD_DIM : (head + 1) * HEAD_DIM, :seen], score_grad
                        )
                    )
                dq_ref[span, :] = jnp.transpose(jnp.concatenate(query_grads, axis=0)) * scale
            bias_ref[...] = jnp.zeros_like(bias_ref)
            for number in range(4):
                span = slice(number * tile, (number + 1) * tile)
                origin = pl.ds(
                    pl.multiple_of(jnp.bitwise_xor(row_ref[0], number) * tile, tile), tile
                )
                turns = (keep_ref[span, :], -lower_ref[span, :], -upper_ref[span, :])
                parts = (
                    turn(dq_ref[span, :], *turns),
                    turn(dk_ref[span, :], *turns),
                    dv_ref[span, :],
                )
                for kind in range(3):
                    low = parts[kind].astype(BF16)
                    low_ref[kind, origin, :] = low
                    bias_ref[kind, 0:1, :] += jnp.sum(low.astype(F32), axis=0, keepdims=True)

        out_ref[...] = low_ref[pl.program_id(1)]
        sum_ref[...] = bias_ref[pl.program_id(1)]

    columns = pl.BlockSpec((seq_len, LANES), lambda h, j: (0, h))
    table = pl.BlockSpec((seq_len, LANES), lambda h, j: (0, 0))
    return pl.pallas_call(
        kernel,
        grid=(pairs, 3),
        in_specs=[smem(), smem()]
        + [columns] * 3
        + [pl.BlockSpec((1, 8, seq_len), lambda h, j: (h, 0, 0))]
        + [columns] * 2
        + [table] * 3,
        out_specs=[
            pl.BlockSpec((seq_len, LANES), lambda h, j: (0, j * pairs + h)),
            pl.BlockSpec((8, LANES), lambda h, j: (0, j * pairs + h)),
        ],
        out_shape=[
            jax.ShapeDtypeStruct((seq_len, 3 * width), BF16),
            jax.ShapeDtypeStruct((8, 3 * width), F32),
        ],
        scratch_shapes=[
            pltpu.VMEM((2, region, region), F32),
            pltpu.VMEM((seq_len, LANES), F32),
            pltpu.VMEM((seq_len, LANES), F32),
            pltpu.VMEM((seq_len, LANES), F32),
            pltpu.VMEM((3, seq_len, LANES), BF16),
            pltpu.VMEM((3, 8, LANES), F32),
        ],
        compiler_params=params(48),
        cost_estimate=cost(
            8 * seq_len * seq_len * width * 4, 20 * seq_len * width, seq_len * seq_len * 2 * pairs
        ),
        name="attend_back",
    )(row, starts, queries, keys, values, logs, outputs, grads, *tables)


def gate_up(rows_two, w_gate):
    tokens, width = rows_two.shape
    tiles = w_gate.shape[1] // (2 * LANES)

    def kernel(in_ref, w_ref, gate_ref, up_ref, hidden_ref):
        both = dot_nn(in_ref[...], w_ref[...])
        gate, up = both[:, :LANES], both[:, LANES:]
        gate_ref[...] = gate.astype(BF16)
        up_ref[...] = up.astype(BF16)
        hidden_ref[...] = (gate * jax.nn.sigmoid(gate) * up).astype(BF16)

    out = pl.BlockSpec((tokens, LANES), lambda i: (0, i))
    return pl.pallas_call(
        kernel,
        grid=(tiles,),
        in_specs=[whole(tokens, width), pl.BlockSpec((width, 2 * LANES), lambda i: (0, i))],
        out_specs=[out] * 3,
        out_shape=[jax.ShapeDtypeStruct((tokens, tiles * LANES), BF16)] * 3,
        compiler_params=params(40),
        cost_estimate=cost(
            2 * tokens * w_gate.size,
            2 * (rows_two.size + w_gate.size) + 6 * tokens * tiles * LANES,
            tokens * tiles * LANES,
        ),
        name="gate_up",
    )(rows_two, w_gate)


def gate_up_back(rows_grad, w_down, gate, up):
    tokens, width = rows_grad.shape
    hidden = w_down.shape[1]
    tile = 256

    def kernel(in_ref, w_ref, gate_ref, up_ref, out_ref):
        pulled = dot_nn(in_ref[...], w_ref[...])
        for number in range(hidden // LANES):
            span = slice(number * LANES, (number + 1) * LANES)
            grad = pulled[:, span]
            gate_part = gate_ref[:, span].astype(F32)
            up_part = up_ref[:, span].astype(F32)
            squash = jax.nn.sigmoid(gate_part)
            first = 2 * number * LANES
            out_ref[:, first : first + LANES] = (
                grad * up_part * squash * (1.0 + gate_part * (1.0 - squash))
            ).astype(BF16)
            out_ref[:, first + LANES : first + 2 * LANES] = (grad * gate_part * squash).astype(BF16)

    return pl.pallas_call(
        kernel,
        grid=(tokens // tile,),
        in_specs=[
            row_blocks(tile, width),
            whole(width, hidden),
            row_blocks(tile, hidden),
            row_blocks(tile, hidden),
        ],
        out_specs=row_blocks(tile, 2 * hidden),
        out_shape=jax.ShapeDtypeStruct((tokens, 2 * hidden), BF16),
        compiler_params=params(40),
        cost_estimate=cost(
            2 * tokens * w_down.size,
            2 * (rows_grad.size + w_down.size) + 8 * tokens * hidden,
            tokens * hidden,
        ),
        name="gate_up_back",
    )(rows_grad, w_down, gate, up)


def adam_update(master, first, second, gradient, keep, rate):
    correction = 1.0 - MOMENT_DECAY**STEP
    new_first = MOMENT_DECAY * first + (1.0 - MOMENT_DECAY) * gradient
    new_second = MOMENT_DECAY * second + (1.0 - MOMENT_DECAY) * gradient * gradient
    direction = new_first / correction / (jnp.sqrt(new_second / correction) + ADAM_EPSILON)
    new_master = master - rate * (direction + WEIGHT_DECAY * master)
    return (
        jnp.where(keep, new_master, master),
        jnp.where(keep, new_first, first),
        jnp.where(keep, new_second, second),
    )


def adam_call(name, keep, states, gradient, rate, grid, state_spec, grad_spec, pieces):
    def kernel(keep_ref, m_ref, f_ref, s_ref, g_ref, mo_ref, fo_ref, so_ref):
        live = keep_ref[LIVE + pl.program_id(0)] > 0
        for state_at, grad_at in pieces:
            results = adam_update(
                m_ref[state_at],
                f_ref[state_at],
                s_ref[state_at],
                g_ref[grad_at].astype(F32),
                live,
                rate,
            )
            mo_ref[state_at], fo_ref[state_at], so_ref[state_at] = results

    return pl.pallas_call(
        kernel,
        grid=grid,
        in_specs=[smem()] + [state_spec] * 3 + [grad_spec],
        out_specs=[state_spec] * 3,
        out_shape=[jax.ShapeDtypeStruct(states[0].shape, F32)] * 3,
        compiler_params=params(58),
        cost_estimate=cost(12 * states[0].size, 26 * states[0].size, states[0].size),
        name=name,
    )(keep, *states, gradient)


def adam_query(keep, states, gradient, rate):
    kinds, rows, width = states[0].shape
    block = rows // CAP
    return adam_call(
        "adam_query",
        keep,
        states,
        gradient,
        rate,
        (CAP,),
        pl.BlockSpec((kinds, block, width), lambda s: (0, s, 0)),
        pl.BlockSpec((1, block, kinds * width), lambda s: (s, 0, 0)),
        [
            ((kind,), (0, slice(None), slice(kind * width, (kind + 1) * width)))
            for kind in range(kinds)
        ],
    )


def adam_flat(name, keep, states, gradient, rate):
    rows, width = states[0].shape
    block = rows // CAP
    return adam_call(
        name,
        keep,
        states,
        gradient,
        rate,
        (CAP,),
        pl.BlockSpec((block, width), lambda s: (s, 0)),
        pl.BlockSpec((1, block, width), lambda s: (s, 0, 0)),
        [((slice(None), slice(None)), (0,))],
    )


def adam_gate(keep, states, gradient, rate):
    block, width = gradient.shape[1:]
    tiles = width // LANES
    pieces = [
        (
            (pl.ds(tile, block, stride=tiles), slice(None)),
            (0, slice(None), slice(tile * LANES, (tile + 1) * LANES)),
        )
        for tile in range(tiles)
    ]
    return adam_call(
        "adam_gate",
        keep,
        states,
        gradient,
        rate,
        (CAP,),
        pl.BlockSpec((block * tiles, LANES), lambda s: (s, 0)),
        pl.BlockSpec((1, block, width), lambda s: (s, 0, 0)),
        pieces,
    )


def matmul(left, right, left_dim, right_dim, dtype):
    return lax.dot_general(
        left, right, (((left_dim,), (right_dim,)), ((), ())), preferred_element_type=F32
    ).astype(dtype)


def flips(axis, reach):
    return [(index, index ^ reach) for index in range(lax.axis_size(axis))]


def x_pairs():
    return flips("row", 1)


def y_pairs():
    return flips("row", 2)


def share_rows(own):
    half = own.shape[0] // 2
    by_x = lax.ppermute(own, "row", x_pairs())
    by_y = lax.ppermute(own, "row", y_pairs())
    top = lax.ppermute(by_x[:half], "row", y_pairs())
    bottom = lax.ppermute(by_y[half:], "row", x_pairs())
    return jnp.concatenate([own, by_x, by_y, top, bottom], axis=0), by_x, by_y


def fold_rows(sums, top, bottom):
    half, width = top.shape

    def kernel(one_ref, two_ref, top_ref, bottom_ref, x_ref, y_ref):
        first = pl.program_id(0) == 0
        one, two = one_ref[...].astype(F32), two_ref[...].astype(F32)
        x_ref[...] = jnp.where(first, one + top_ref[...].astype(F32), one).astype(BF16)
        y_ref[...] = jnp.where(first, two, two + bottom_ref[...].astype(F32)).astype(BF16)

    out = jax.ShapeDtypeStruct((2 * half, width), BF16)
    return pl.pallas_call(
        kernel,
        grid=(2,),
        in_specs=[
            row_blocks(half, width, 2),
            row_blocks(half, width, 4),
            whole(half, width),
            whole(half, width),
        ],
        out_specs=[row_blocks(half, width)] * 2,
        out_shape=[out, out],
        compiler_params=params(),
        cost_estimate=cost(0, 10 * half * width),
        name="fold_rows",
    )(sums, sums, top, bottom)


def scatter_rows(sums, *others):
    rows = sums.shape[0] // 4
    half = rows // 2
    top = lax.ppermute(sums[3 * rows : 3 * rows + half], "row", y_pairs())
    bottom = lax.ppermute(sums[3 * rows + half :], "row", x_pairs())
    if others:
        top = after(top, *others)
    to_x, to_y = fold_rows(sums, top, bottom)
    return (
        (sums, lax.ppermute(to_x, "row", x_pairs()), lax.ppermute(to_y, "row", y_pairs())),
        to_x,
        to_y,
    )


def chip_moves(columns, moves):
    chips = columns // 2
    return [
        (2 * chip + core, 2 * (chip + moves[core]) + core)
        for chip in range(chips)
        for core in range(2)
        if 0 <= chip + moves[core] < chips
    ]


def swap_cores(values, columns):
    return lax.ppermute(values, "col", [(index, index ^ 1) for index in range(columns)])


def both_cores(values, columns):
    return values, swap_cores(values, columns)


def local_line(
    inputs,
    cotangent,
    image_starts,
    owners,
    query_master,
    query_first,
    query_second,
    output_master,
    output_first,
    output_second,
    gate_master,
    gate_first,
    gate_second,
    down_master,
    down_first,
    down_second,
    vector_master,
    vector_first,
    vector_second,
):
    columns = lax.axis_size("col")
    col_index = lax.axis_index("col")
    row_index = lax.axis_index("row")
    blocks = owners.shape[0]
    block_rows = D // blocks
    head_blocks = query_master.shape[2] // LANES
    codes, order, sorted_slots, head_slots, head_places = plan_blocks(
        owners, jnp.stack([col_index, row_index]), columns, head_blocks
    )
    uneven = codes[UNEVEN]

    inward = chip_moves(columns, (1, -1))
    outward = chip_moves(columns, (-1, 1))

    def spread_out(own, send_codes, keep_codes):
        partner = swap_cores(own, columns)
        sent = pick_blocks(send_codes, 0, 2, [own, partner])
        near = lax.ppermute(sent, "col", inward)

        def near_only():
            return pick_blocks(keep_codes, 4, 2, [own, partner, near])

        def farther(first, count):
            more = pick_blocks(codes, first, count, [own, partner])
            return pick_blocks(
                keep_codes, 4, 2, [own, partner, near, lax.ppermute(more, "col", outward)]
            )

        kept = lax.switch(
            uneven, [near_only, lambda: farther(UNEVEN + 1, 1), lambda: farther(2, 2)]
        )
        return sent, kept.reshape(2 * block_rows, own.shape[2])

    def gather(part):
        return lax.all_gather(part, "col", axis=0, tiled=True)

    def sum_up(gradient):
        own = lax.psum_scatter(gradient, "col", scatter_dimension=0, tiled=True)
        return own.reshape(2, block_rows, own.shape[1])

    def start_home(own):
        return own, lax.ppermute(own, "col", outward)

    def finish_home(own, near, codes):
        held = [own, near, swap_cores(own, columns), swap_cores(near, columns)]

        def near_only():
            return pick_blocks(codes, 6, CAP, held)

        def farther(more):
            far = lax.ppermute(more, "col", inward)
            return pick_blocks(codes, 6, CAP, held + [far, swap_cores(far, columns)])

        def one_farther():
            return farther(lax.dynamic_slice_in_dim(own, 1 - col_index % 2, 1, 0))

        return lax.switch(uneven, [near_only, one_farther, lambda: farther(own)])

    local_in = inputs[0]
    upstream = cotangent[0]
    row = row_index.reshape(1)
    tables = lane_tables(inputs.shape[1] * 4)
    rates = step_rates()

    query_slabs = [
        jnp.transpose(part, (1, 0, 2)) for part in (query_master, query_first, query_second)
    ]
    query_width = 3 * query_slabs[0].shape[2]
    sent_attention, attention_part = spread_out(
        pack_attention(query_slabs[0], output_master), codes, codes
    )
    plain_one = norm_one(after(order, sent_attention), local_in)
    rows_plain, *plain_parts = share_rows(plain_one)
    w_attention = gather(attention_part)
    w_query, w_output = w_attention[:, :query_width], w_attention[:, query_width:]
    vector_rows = jnp.pad(vector_master.T, ((0, 9), (0, 0))).astype(BF16)
    vector_blocks = jnp.transpose(vector_rows.reshape(16, CAP, block_rows), (1, 0, 2))
    vectors, bias = spread_vectors(
        sorted_slots, head_slots, gather(after(vector_blocks, attention_part, *plain_parts))
    )
    gate_states = [gate_lines(part) for part in (gate_master, gate_first, gate_second)]
    rows_grad = share_rows(order_grad(after(order, rows_plain), upstream))[0]
    rows_one = scale_rows(rows_plain, vectors)
    unused, gate_part = spread_out(
        pack_gate(gate_states[0], gate_master.shape[0]),
        after(codes, vectors),
        after(codes, rows_grad, rows_one),
    )
    w_gate = gather(gate_part)
    mixed = matmul(rows_one, w_query, 1, 0, F32)
    unused, down_part = spread_out(
        pack_flat("pack_down", down_master), after(codes, gate_part), after(codes, mixed)
    )
    w_down = gather(down_part)
    attended, queries, keys, values, logs = attend(
        after(row, down_part), image_starts, mixed, bias, tables
    )
    middle, normed_two = norm_two(
        order, local_in, scatter_rows(matmul(attended, w_output, 1, 1, BF16))[0], vectors
    )
    rows_two = share_rows(normed_two)[0]
    gate, up, hidden = gate_up(rows_two, w_gate)

    down_sums = matmul(rows_grad, hidden, 0, 0, BF16)
    down_own = sum_up(down_sums)
    gate_up_grad = gate_up_back(rows_grad, w_down, after(gate, down_sums), up)
    pulled_two = matmul(gate_up_grad, w_gate, 1, 1, BF16)
    gate_sums = matmul(rows_two, after(gate_up_grad, pulled_two), 0, 0, BF16)
    gate_own = sum_up(gate_sums)
    out_sums = matmul(after(hidden, gate_sums), w_down, 1, 1, BF16)
    middle_grad, low_middle, sums_two = norm_two_back(
        order, upstream, middle, scatter_rows(pulled_two)[0], after(vectors, gate_sums, out_sums)
    )
    rows_mid = share_rows(low_middle)[0]
    down_home = start_home(after(down_own, low_middle))
    attended_grad = matmul(rows_mid, w_output, 1, 0, BF16)
    output_sums = matmul(rows_mid, after(attended, attended_grad), 0, 0, BF16)
    output_own = sum_up(output_sums)
    out_partial, *out_parts = scatter_rows(after(out_sums, rows_mid), output_sums)
    mixed_grad, bias_sums = attend_back(
        after(row, *out_parts),
        image_starts,
        queries,
        keys,
        values,
        logs,
        attended,
        attended_grad,
        tables,
    )
    layer_out = finish_out(order, after(middle, mixed_grad), out_partial)
    pulled_one = matmul(after(mixed_grad, layer_out), w_query, 1, 1, BF16)
    query_sums = matmul(rows_one, after(mixed_grad, pulled_one, down_home[1]), 0, 0, BF16)
    query_own = sum_up(query_sums)
    gate_home = start_home(after(gate_own, query_sums))
    new_down = adam_flat(
        "adam_down",
        codes,
        (down_master, down_first, down_second),
        finish_home(*down_home, after(codes, query_sums)),
        rates[3],
    )
    input_grad, sums_one = norm_one_back(
        order,
        local_in,
        middle_grad,
        scatter_rows(pulled_one)[0],
        after(vectors, new_down[0]),
    )
    vector_sums = place_vector_grads(head_places, sums_one, sums_two, bias_sums)
    for axis, reach in (("row", 1), ("row", 2), ("col", 1), ("col", 2), ("col", 4)):
        vector_sums = vector_sums + lax.ppermute(vector_sums, axis, flips(axis, reach))
    new_gate = [
        gate_unlines(part, gate_master.shape)
        for part in adam_gate(
            codes,
            gate_states,
            finish_home(gate_home[0], after(gate_home[1], input_grad), codes),
            rates[2],
        )
    ]
    output_home = start_home(after(output_own, input_grad))
    new_output = adam_flat(
        "adam_output",
        codes,
        (output_master, output_first, output_second),
        finish_home(output_home[0], after(output_home[1], new_gate[0]), codes),
        rates[1],
    )
    new_vector = [
        part.T
        for part in adam_vector(
            codes,
            [part.T for part in (vector_master, vector_first, vector_second)],
            vector_sums,
            rates[4],
        )
    ]
    query_own = after(query_own, new_output[0], new_vector[0])
    new_query = [
        jnp.transpose(part, (1, 0, 2))
        for part in adam_query(
            codes, query_slabs, finish_home(*start_home(query_own), codes), rates[0]
        )
    ]
    return (
        layer_out[None],
        input_grad[None],
        *new_query,
        *new_output,
        *new_gate,
        *new_down,
        *new_vector,
    )


def solution(mesh):
    one_hop_line = mesh.shape["row"] == 4 and mesh.shape["col"] == 8
    return jax.shard_map(
        local_line if one_hop_line else local,
        mesh=mesh,
        in_specs=(
            P("col", "row", None),
            P("col", "row", None),
            P("col", None),
            P(),
            P("col", None, "row"),
            P("col", None, "row"),
            P("col", None, "row"),
            P("col", "row"),
            P("col", "row"),
            P("col", "row"),
            P("col", None, "row"),
            P("col", None, "row"),
            P("col", None, "row"),
            P("col", "row"),
            P("col", "row"),
            P("col", "row"),
            P("col", None),
            P("col", None),
            P("col", None),
        ),
        out_specs=(
            P("col", "row", None),
            P("col", "row", None),
            P("col", None, "row"),
            P("col", None, "row"),
            P("col", None, "row"),
            P("col", "row"),
            P("col", "row"),
            P("col", "row"),
            P("col", None, "row"),
            P("col", None, "row"),
            P("col", None, "row"),
            P("col", "row"),
            P("col", "row"),
            P("col", "row"),
            P("col", None),
            P("col", None),
            P("col", None),
        ),
        check_vma=False,
    )
```

profile of v0, /device:TPU:0, one launch (start us, length us, event | category | flops | bytes accessed | tf_op | source)
XLA Modules:
  0.0 677.7 jit_solution(11325630546658094106)
XLA Ops:
  22.4 11.0 %collective-permute-done.27 = bf16[2,128,2048]{2,1,0:T(8,128)(2,1)S(1)} collective-permute-done((bf16[2,128,2048]{2,1,0:T(8,128)(2,1)S(1)}, bf16[2,128,2048]{2,1,0:T(8,128)(2,1)S(1)}, u32[]{:S(2)}, u32[]{:S(2)}) %collective-permute-start.27) | collective-permute-done | bytes 1048608 | tf_op jit(solution)/shard_map/ppermute | solution.py:1506
  45.6 16.0 %collective-permute-done.23 = bf16[256,2048]{1,0:T(8,128)(2,1)S(1)} collective-permute-done((bf16[256,2048]{1,0:T(8,128)(2,1)S(1)}, bf16[256,2048]{1,0:T(8,128)(2,1)S(1)}, u32[]{:S(2)}, u32[]{:S(2)}) %collective-permute-start.23) | collective-permute-done | bytes 1048608 | tf_op jit(solution)/shard_map/ppermute | solution.py:1401
  70.9 10.0 %collective-permute-done.25 = bf16[128,2048]{1,0:T(8,128)(2,1)S(1)} collective-permute-done((bf16[128,2048]{1,0:T(8,128)(2,1)S(1)}, bf16[128,2048]{1,0:T(8,128)(2,1)S(1)}, u32[]{:S(2)}, u32[]{:S(2)}) %collective-permute-start.25) | collective-permute-done | bytes 524320 | tf_op jit(solution)/shard_map/ppermute | solution.py:1403
  86.6 15.4 %all_gather.12.in_ref = bf16[32,16,128]{2,1,0:T(8,128)(2,1)S(1)} all-gather(bf16[4,16,128]{2,1,0:T(8,128)(2,1)S(1)} %bitcast_bitcast_fusion), channel_id=1, replica_groups=mesh['row'=4,'col'=8] {'col'}, dimensions={0}, use_global_device_ids=true | all-gather | bytes 147456 | tf_op jit(solution)/shard_map/all_gather | solution.py:1523
  111.9 8.1 %collective-permute-done.31 = bf16[128,2048]{1,0:T(8,128)(2,1)S(1)} collective-permute-done((bf16[128,2048]{1,0:T(8,128)(2,1)S(1)}, bf16[128,2048]{1,0:T(8,128)(2,1)S(1)}, u32[]{:S(2)}, u32[]{:S(2)}) %collective-permute-start.31) | collective-permute-done | bytes 524320 | tf_op jit(solution)/shard_map/ppermute | solution.py:1403
  122.5 8.0 %collective-permute-done.34 = bf16[2,128,2816]{2,1,0:T(8,128)(2,1)S(1)} collective-permute-done((bf16[2,128,2816]{2,1,0:T(8,128)(2,1)S(1)}, bf16[2,128,2816]{2,1,0:T(8,128)(2,1)S(1)}, u32[]{:S(2)}, u32[]{:S(2)}) %collective-permute-start.34) | collective-permute-done | bytes 1441824 | tf_op jit(solution)/shard_map/ppermute | solution.py:1506
  145.8 12.0 %fusion.2.q_ref.k_ref.v_ref = f32[1024,1536]{1,0:T(8,128)} fusion(bf16[1024,2048]{1,0:T(8,128)(2,1)} %copy-done.14, bf16[2048,2048]{1,0:T(8,128)(2,1)} %all-gather.4.cloned.1.call-done), kind=kOutput, calls=%fused_computation.9 | convolution fusion | flops 6442450944 | bytes 16777216 | tf_op jit(solution)/shard_map/dot_general | solution.py:1382
  157.8 11.4 %collective-permute-done.35 = bf16[2,128,1408]{2,1,0:T(8,128)(2,1)} collective-permute-done((bf16[2,128,1408]{2,1,0:T(8,128)(2,1)S(1)}, bf16[2,128,1408]{2,1,0:T(8,128)(2,1)}, u32[]{:S(2)}, u32[]{:S(2)}) %collective-permute-start.35) | collective-permute-done | bytes 720928 | tf_op jit(solution)/shard_map/ppermute | solution.py:1506
  176.2 22.8 %attend.1 = (bf16[1024,512]{1,0:T(8,128)(2,1)S(1)}, bf16[1024,512]{1,0:T(8,128)(2,1)S(1)}, bf16[1024,512]{1,0:T(8,128)(2,1)S(1)}, bf16[1024,512]{1,0:T(8,128)(2,1)S(1)}, f32[4,8,1024]{2,1,0:T(8,128)S(1)}) custom-call(s32[1]{0:T(128)} %bitcast.10.row_ref, s32[1,2]{1,0:T(1,128)S(1)} %copy-done.29, f32[1024,1536]{1,0:T(8,128)S(1)} %copy-done.40, ...), custom_call_target="tpu_custom_call" | custom-call | flops 6442450944 | bytes 10485760 | tf_op jit(solution)/shard_map/attend/pallas_call | solution.py:1075
  218.1 18.4 %collective-permute-done.38.x_ref = bf16[256,2048]{1,0:T(8,128)(2,1)S(1)} collective-permute-done((bf16[256,2048]{1,0:T(8,128)(2,1)S(1)}, bf16[256,2048]{1,0:T(8,128)(2,1)S(1)}, u32[]{:S(2)}, u32[]{:S(2)}) %collective-permute-start.38) | collective-permute-done | bytes 1048608 | tf_op jit(solution)/shard_map/ppermute | solution.py:1444
  242.3 18.3 %collective-permute-done.40 = bf16[256,2048]{1,0:T(8,128)(2,1)S(1)} collective-permute-done((bf16[256,2048]{1,0:T(8,128)(2,1)S(1)}, bf16[256,2048]{1,0:T(8,128)(2,1)S(1)}, u32[]{:S(2)}, u32[]{:S(2)}) %collective-permute-start.40) | collective-permute-done | bytes 1048608 | tf_op jit(solution)/shard_map/ppermute | solution.py:1401
  263.1 12.5 %collective-permute-done.42 = bf16[128,2048]{1,0:T(8,128)(2,1)S(1)} collective-permute-done((bf16[128,2048]{1,0:T(8,128)(2,1)S(1)}, bf16[128,2048]{1,0:T(8,128)(2,1)S(1)}, u32[]{:S(2)}, u32[]{:S(2)}) %collective-permute-start.42) | collective-permute-done | bytes 524320 | tf_op jit(solution)/shard_map/ppermute | solution.py:1403
  280.1 16.7 %gate_up.1 = (bf16[1024,1408]{1,0:T(8,128)(2,1)S(1)}, bf16[1024,1408]{1,0:T(8,128)(2,1)S(1)}, bf16[1024,1408]{1,0:T(8,128)(2,1)S(1)}) custom-call(bf16[1024,2048]{1,0:T(8,128)(2,1)S(1)} %copy-done.22, bf16[2048,2816]{1,0:T(8,128)(2,1)} %all-gather.6.cloned.1.call-done.w_ref), custom_call_target="tpu_custom_call" | custom-call | flops 11811160064 | bytes 24379392 | tf_op jit(solution)/shard_map/gate_up/pallas_call | solution.py:1228
  301.6 8.9 %convolution_convert_fusion.2 = bf16[2048,1408]{1,0:T(8,128)(2,1)} fusion(bf16[1024,2048]{1,0:T(8,128)(2,1)S(1)} %copy-done.19, bf16[1024,1408]{1,0:T(8,128)(2,1)S(1)} %get-tuple-element.458), kind=kOutput, calls=%fused_computation.6 | convolution fusion | flops 5908463616 | bytes 12845056 | tf_op jit(solution)/shard_map/dot_general | solution.py:1382
  317.1 12.2 %gate_up_back.1 = bf16[1024,2816]{1,0:T(8,128)(2,1)} custom-call(bf16[1024,2048]{1,0:T(8,128)(2,1)S(1)} %copy-done.20, bf16[2048,1408]{1,0:T(8,128)(2,1)} %all-gather.8.cloned.1.call-done.w_ref, bf16[1024,1408]{1,0:T(8,128)(2,1)S(1)} %copy-done.37, bf16[1024,1408]{1,0:T(8,128)(2,1)S(1)} %copy-done.39), custom_call_target="tpu_custom_call" | custom-call | flops 5905580032 | bytes 21495808 | tf_op jit(solution)/shard_map/gate_up_back/pallas_call | solution.py:1263
  329.3 18.1 %convolution_convert_fusion.3.one_ref.two_ref.own_ref = bf16[1024,2048]{1,0:T(8,128)(2,1)} fusion(bf16[1024,2816]{1,0:T(8,128)(2,1)} %gate_up_back.1, bf16[2048,2816]{1,0:T(8,128)(2,1)} %all-gather.6.cloned.1.call-done.w_ref), kind=kOutput, calls=%fused_computation.11 | convolution fusion | flops 11813257216 | bytes 21495808 | tf_op jit(solution)/shard_map/dot_general | solution.py:1382
  347.4 15.1 %convolution_convert_fusion = bf16[2048,2816]{1,0:T(8,128)(2,1)} fusion(bf16[1024,2048]{1,0:T(8,128)(2,1)S(1)} %copy-done.23, bf16[1024,2816]{1,0:T(8,128)(2,1)S(1)} %copy-done.63), kind=kOutput, calls=%fused_computation.4 | convolution fusion | flops 11816927232 | bytes 21495808 | tf_op jit(solution)/shard_map/dot_general | solution.py:1382
  379.8 9.5 %convolution_convert_fusion.4.one_ref.two_ref.own_ref = bf16[1024,2048]{1,0:T(8,128)(2,1)S(1)} fusion(bf16[1024,1408]{1,0:T(8,128)(2,1)S(1)} %copy-done.51, bf16[2048,1408]{1,0:T(8,128)(2,1)} %all-gather.8.cloned.1.call-done.w_ref), kind=kOutput, calls=%fused_computation.13 | convolution fusion | flops 5907677184 | bytes 12845056 | tf_op jit(solution)/shard_map/dot_general | solution.py:1382
  389.3 7.4 %collective-permute-done.46.x_ref = bf16[256,2048]{1,0:T(8,128)(2,1)S(1)} collective-permute-done((bf16[256,2048]{1,0:T(8,128)(2,1)S(1)}, bf16[256,2048]{1,0:T(8,128)(2,1)S(1)}, u32[]{:S(2)}, u32[]{:S(2)}) %collective-permute-start.46) | collective-permute-done | bytes 1048608 | tf_op jit(solution)/shard_map/ppermute | solution.py:1444
  404.2 18.2 %collective-permute-done.48 = bf16[256,2048]{1,0:T(8,128)(2,1)S(1)} collective-permute-done((bf16[256,2048]{1,0:T(8,128)(2,1)S(1)}, bf16[256,2048]{1,0:T(8,128)(2,1)S(1)}, u32[]{:S(2)}, u32[]{:S(2)}) %collective-permute-start.48) | collective-permute-done | bytes 1048608 | tf_op jit(solution)/shard_map/ppermute | solution.py:1401
  425.0 12.3 %collective-permute-done.50 = bf16[128,2048]{1,0:T(8,128)(2,1)S(1)} collective-permute-done((bf16[128,2048]{1,0:T(8,128)(2,1)S(1)}, bf16[128,2048]{1,0:T(8,128)(2,1)S(1)}, u32[]{:S(2)}, u32[]{:S(2)}) %collective-permute-start.50) | collective-permute-done | bytes 524320 | tf_op jit(solution)/shard_map/ppermute | solution.py:1403
  449.5 6.8 %collective-permute-done.52.top_ref = bf16[128,2048]{1,0:T(8,128)(2,1)S(1)} collective-permute-done((bf16[128,2048]{1,0:T(8,128)(2,1)}, bf16[128,2048]{1,0:T(8,128)(2,1)S(1)}, u32[]{:S(2)}, u32[]{:S(2)}) %collective-permute-start.52) | collective-permute-done | bytes 524320 | tf_op jit(solution)/shard_map/ppermute | solution.py:1438
  464.2 26.8 %attend_back.1 = (bf16[1024,1536]{1,0:T(8,128)(2,1)}, f32[8,1536]{1,0:T(8,128)S(1)}) custom-call(s32[1]{0:T(128)} %bitcast.10.row_ref, s32[1,2]{1,0:T(1,128)S(1)} %copy-done.29, bf16[1024,512]{1,0:T(8,128)(2,1)S(1)} %copy-done.45, bf16[1024,512]{1,0:T(8,128)(2,1)S(1)} %copy-done.47, bf16[1024,512]{1,0:T(8,128)(2,1)S(1)} %copy-done.49, ...), custom_call_target="tpu_custom_call" | custom-call | flops 17179869184 | bytes 10485760 | tf_op jit(solution)/shard_map/attend_back/pallas_call | solution.py:1184
  495.1 11.8 %fusion.4.one_ref.two_ref.own_ref = bf16[1024,2048]{1,0:T(8,128)(2,1)} fusion(bf16[1024,1536]{1,0:T(8,128)(2,1)} %get-tuple-element.480, bf16[2048,2048]{1,0:T(8,128)(2,1)} %all-gather.4.cloned.1.call-done), kind=kOutput, calls=%fused_computation.12 | convolution fusion | flops 6444548096 | bytes 13631488 | tf_op jit(solution)/shard_map/dot_general | solution.py:1382
  506.9 19.7 %collective-permute-done.60 = bf16[2,128,1408]{2,1,0:T(8,128)(2,1)} collective-permute-done((bf16[2,128,1408]{2,1,0:T(8,128)(2,1)}, bf16[2,128,1408]{2,1,0:T(8,128)(2,1)}, u32[]{:S(2)}, u32[]{:S(2)}) %collective-permute-start.60) | collective-permute-done | bytes 720928 | tf_op jit(solution)/shard_map/ppermute | solution.py:1530
  526.6 8.7 %convolution_convert_fusion.1 = bf16[2048,1536]{1,0:T(8,128)(2,1)} fusion(bf16[1024,2048]{1,0:T(8,128)(2,1)S(1)} %copy-done.15, bf16[1024,1536]{1,0:T(8,128)(2,1)S(1)} %copy-done.64), kind=kOutput, calls=%fused_computation.5 | convolution fusion | flops 6445596672 | bytes 13631488 | tf_op jit(solution)/shard_map/dot_general | solution.py:1382
  559.4 8.7 %adam_down.1 = (f32[512,1408]{1,0:T(8,128)}, f32[512,1408]{1,0:T(8,128)}, f32[512,1408]{1,0:T(8,128)}) custom-call(s32[32]{0:T(128)} %copy-done.62, f32[512,1408]{1,0:T(8,128)} %m_ref.2, f32[512,1408]{1,0:T(8,128)} %f_ref.2, f32[512,1408]{1,0:T(8,128)} %s_ref.2, bf16[4,128,1408]{2,1,0:T(8,128)(2,1)} %get-tuple-element.519.g_ref), custom_call_target="tpu_custom_call" | custom-call | flops 8650752 | bytes 18743296 | tf_op jit(solution)/shard_map/adam_down/pallas_call | solution.py:1311
  591.0 13.8 %adam_gate.1 = (f32[11264,128]{1,0:T(8,128)}, f32[11264,128]{1,0:T(8,128)}, f32[11264,128]{1,0:T(8,128)}) custom-call(s32[32]{0:T(128)} %copy-done.62, f32[11264,128]{1,0:T(8,128)} %bitcast.95, f32[11264,128]{1,0:T(8,128)} %bitcast.111, f32[11264,128]{1,0:T(8,128)} %bitcast.112, bf16[4,128,2816]{2,1,0:T(8,128)(2,1)} %get-tuple-element.520.g_ref), custom_call_target="tpu_custom_call" | custom-call | flops 17301504 | bytes 37486592 | tf_op jit(solution)/shard_map/adam_gate/pallas_call | solution.py:1311
  616.2 8.4 %collective-permute-done.73 = f32[8,2048]{1,0:T(8,128)S(1)} collective-permute-done((f32[8,2048]{1,0:T(8,128)S(1)}, f32[8,2048]{1,0:T(8,128)S(1)}, u32[]{:S(2)}, u32[]{:S(2)}) %collective-permute-start.73) | collective-permute-done | bytes 65568 | tf_op jit(solution)/shard_map/ppermute | solution.py:1640
  631.9 10.1 %reduce-scatter.7.cloned.1.call-done = bf16[256,1536]{1,0:T(8,128)(2,1)} async-done(((bf16[2048,1536]{1,0:T(8,128)(2,1)}), bf16[256,1536]{1,0:T(8,128)(2,1)}) %reduce-scatter.7.cloned.1.call-update) | async-done | bytes 786448 | tf_op jit(solution)/shard_map/reduce_scatter | solution.py:1526
  643.5 12.5 %collective-permute-done.74 = bf16[2,128,1536]{2,1,0:T(8,128)(2,1)S(1)} collective-permute-done((bf16[2,128,1536]{2,1,0:T(8,128)(2,1)}, bf16[2,128,1536]{2,1,0:T(8,128)(2,1)S(1)}, u32[]{:S(2)}, u32[]{:S(2)}) %collective-permute-start.74) | collective-permute-done | bytes 786464 | tf_op jit(solution)/shard_map/ppermute | solution.py:1530
  661.4 9.1 %adam_query.1 = (f32[3,512,512]{2,1,0:T(8,128)}, f32[3,512,512]{2,1,0:T(8,128)}, f32[3,512,512]{2,1,0:T(8,128)}) custom-call(s32[32]{0:T(128)} %copy-done.62, f32[3,512,512]{2,1,0:T(8,128)} %bitcast.97, f32[3,512,512]{2,1,0:T(8,128)} %bitcast.121, f32[3,512,512]{2,1,0:T(8,128)} %bitcast.122, bf16[4,128,1536]{2,1,0:T(8,128)(2,1)} %get-tuple-element.522.g_ref), custom_call_target="tpu_custom_call" | custom-call | flops 9437184 | bytes 20447232 | tf_op jit(solution)/shard_map/adam_query/pallas_call | solution.py:1311
  (320 shorter events, 260.1 us)
Async XLA Ops:
  7.2 138.6 %all-gather.4.cloned.1.call-start = ((), (), s32[]{:S(2)}) async-start(), calls=%async_computation.4 | async-start | bytes 9437184 | tf_op jit(solution)/shard_map/all_gather | solution.py:1523
  36.2 241.7 %all-gather.6.cloned.1.call-start = ((), (), s32[]{:S(2)}) async-start(), calls=%async_computation.5 | async-start | bytes 12976128 | tf_op jit(solution)/shard_map/all_gather | solution.py:1523
  37.7 23.9 %collective-permute-start.23 = (bf16[256,2048]{1,0:T(8,128)(2,1)S(1)}, bf16[256,2048]{1,0:T(8,128)(2,1)S(1)}, u32[]{:S(2)}, u32[]{:S(2)}) collective-permute-start(bf16[256,2048]{1,0:T(8,128)(2,1)S(1)} %norm_one.1), channel_id=1, source_target_pairs={{0,8},{8,0},{16,24},{24,16},{1,9},{9,1},{17,25},{25,17},{2,10},{10... | collective-permute-start | bytes 3145736 | tf_op jit(solution)/shard_map/ppermute | solution.py:1401
  44.1 58.5 %collective-permute-start.33 = (bf16[4,128,2816]{2,1,0:T(8,128)(2,1)}, bf16[4,128,2816]{2,1,0:T(8,128)(2,1)S(1)}, u32[]{:S(2)}, u32[]{:S(2)}) collective-permute-start(bf16[4,128,2816]{2,1,0:T(8,128)(2,1)} %pack_gate.1.refs_0_), channel_id=1, source_target_pairs={{0,1},{1,0},{2,3},{3,2},{4,5},{5,4},{6,7},{7,6},{8,9},{9,8},{10,11... | collective-permute-start | bytes 8650760 | tf_op jit(solution)/shard_map/ppermute | solution.py:1461
  44.1 26.0 %collective-permute-start.24 = (bf16[256,2048]{1,0:T(8,128)(2,1)S(1)}, bf16[256,2048]{1,0:T(8,128)(2,1)S(1)}, u32[]{:S(2)}, u32[]{:S(2)}) collective-permute-start(bf16[256,2048]{1,0:T(8,128)(2,1)S(1)} %norm_one.1), channel_id=1, source_target_pairs={{0,16},{8,24},{16,0},{24,8},{1,17},{9,25},{17,1},{25,9},{2,18},{10... | collective-permute-start | bytes 3145736 | tf_op jit(solution)/shard_map/ppermute | solution.py:1402
  61.6 19.3 %collective-permute-start.25 = (bf16[128,2048]{1,0:T(8,128)(2,1)S(1)}, bf16[128,2048]{1,0:T(8,128)(2,1)S(1)}, u32[]{:S(2)}, u32[]{:S(2)}) collective-permute-start(bf16[128,2048]{1,0:T(8,128)(2,1)S(1)} %slice.76), channel_id=1, source_target_pairs={{0,16},{8,24},{16,0},{24,8},{1,17},{9,25},{17,1},{25,9},{2,18},{10... | collective-permute-start | bytes 1572872 | tf_op jit(solution)/shard_map/ppermute | solution.py:1403
  84.4 23.8 %collective-permute-start.29 = (bf16[256,2048]{1,0:T(8,128)(2,1)S(1)}, bf16[256,2048]{1,0:T(8,128)(2,1)S(1)}, u32[]{:S(2)}, u32[]{:S(2)}) collective-permute-start(bf16[256,2048]{1,0:T(8,128)(2,1)S(1)} %order_grad.1), channel_id=1, source_target_pairs={{0,8},{8,0},{16,24},{24,16},{1,9},{9,1},{17,25},{25,17},{2,10},{10... | collective-permute-start | bytes 3145736 | tf_op jit(solution)/shard_map/ppermute | solution.py:1401
  85.0 26.0 %collective-permute-start.30 = (bf16[256,2048]{1,0:T(8,128)(2,1)S(1)}, bf16[256,2048]{1,0:T(8,128)(2,1)S(1)}, u32[]{:S(2)}, u32[]{:S(2)}) collective-permute-start(bf16[256,2048]{1,0:T(8,128)(2,1)S(1)} %order_grad.1), channel_id=1, source_target_pairs={{0,16},{8,24},{16,0},{24,8},{1,17},{9,25},{17,1},{25,9},{2,18},{10... | collective-permute-start | bytes 3145736 | tf_op jit(solution)/shard_map/ppermute | solution.py:1402
  103.8 26.8 %collective-permute-start.34 = (bf16[2,128,2816]{2,1,0:T(8,128)(2,1)S(1)}, bf16[2,128,2816]{2,1,0:T(8,128)(2,1)S(1)}, u32[]{:S(2)}, u32[]{:S(2)}) collective-permute-start(bf16[2,128,2816]{2,1,0:T(8,128)(2,1)S(1)} %pick_blocks.58), channel_id=1, source_target_pairs={{0,2},{2,4},{3,1},{4,6},{5,3},{7,5},{8,10},{10,12},{11,9},{12,14},... | collective-permute-start | bytes 4325384 | tf_op jit(solution)/shard_map/ppermute | solution.py:1506
  132.9 178.4 %all-gather.8.cloned.1.call-start = ((), (), s32[]{:S(2)}) async-start(), calls=%async_computation.6 | async-start | bytes 6488064 | tf_op jit(solution)/shard_map/all_gather | solution.py:1523
  140.6 28.6 %collective-permute-start.35 = (bf16[2,128,1408]{2,1,0:T(8,128)(2,1)S(1)}, bf16[2,128,1408]{2,1,0:T(8,128)(2,1)}, u32[]{:S(2)}, u32[]{:S(2)}) collective-permute-start(bf16[2,128,1408]{2,1,0:T(8,128)(2,1)S(1)} %pick_blocks.59), channel_id=1, source_target_pairs={{0,2},{2,4},{3,1},{4,6},{5,3},{7,5},{8,10},{10,12},{11,9},{12,14},... | collective-permute-start | bytes 2162696 | tf_op jit(solution)/shard_map/ppermute | solution.py:1506
  171.0 322.6 %reduce-scatter.5.cloned.1.call-start = ((), (), s32[]{:S(2)}) async-start(), calls=%async_computation.7 | async-start | bytes 6488064 | tf_op jit(solution)/shard_map/reduce_scatter | solution.py:1526
  216.0 20.5 %collective-permute-start.38 = (bf16[256,2048]{1,0:T(8,128)(2,1)S(1)}, bf16[256,2048]{1,0:T(8,128)(2,1)S(1)}, u32[]{:S(2)}, u32[]{:S(2)}) collective-permute-start(bf16[256,2048]{1,0:T(8,128)(2,1)S(1)} %get-tuple-element.449), channel_id=1, source_target_pairs={{0,8},{8,0},{16,24},{24,16},{1,9},{9,1},{17,25},{25,17},{2,10},{10... | collective-permute-start | bytes 3145736 | tf_op jit(solution)/shard_map/ppermute | solution.py:1444
  216.7 20.8 %collective-permute-start.39 = (bf16[256,2048]{1,0:T(8,128)(2,1)S(1)}, bf16[256,2048]{1,0:T(8,128)(2,1)S(1)}, u32[]{:S(2)}, u32[]{:S(2)}) collective-permute-start(bf16[256,2048]{1,0:T(8,128)(2,1)S(1)} %get-tuple-element.450), channel_id=1, source_target_pairs={{0,16},{8,24},{16,0},{24,8},{1,17},{9,25},{17,1},{25,9},{2,18},{10... | collective-permute-start | bytes 3145736 | tf_op jit(solution)/shard_map/ppermute | solution.py:1444
  239.5 21.1 %collective-permute-start.40 = (bf16[256,2048]{1,0:T(8,128)(2,1)S(1)}, bf16[256,2048]{1,0:T(8,128)(2,1)S(1)}, u32[]{:S(2)}, u32[]{:S(2)}) collective-permute-start(bf16[256,2048]{1,0:T(8,128)(2,1)S(1)} %get-tuple-element.452), channel_id=1, source_target_pairs={{0,8},{8,0},{16,24},{24,16},{1,9},{9,1},{17,25},{25,17},{2,10},{10... | collective-permute-start | bytes 3145736 | tf_op jit(solution)/shard_map/ppermute | solution.py:1401
  240.8 21.4 %collective-permute-start.41 = (bf16[256,2048]{1,0:T(8,128)(2,1)S(1)}, bf16[256,2048]{1,0:T(8,128)(2,1)S(1)}, u32[]{:S(2)}, u32[]{:S(2)}) collective-permute-start(bf16[256,2048]{1,0:T(8,128)(2,1)S(1)} %get-tuple-element.452), channel_id=1, source_target_pairs={{0,16},{8,24},{16,0},{24,8},{1,17},{9,25},{17,1},{25,9},{2,18},{10... | collective-permute-start | bytes 3145736 | tf_op jit(solution)/shard_map/ppermute | solution.py:1402
  310.5 228.2 %reduce-scatter.11.cloned.1.call-start = ((), (), s32[]{:S(2)}) async-start(), calls=%async_computation.10 | async-start | bytes 12976128 | tf_op jit(solution)/shard_map/reduce_scatter | solution.py:1526
  362.6 216.9 %reduce-scatter.9.cloned.1.call-start = ((), (), s32[]{:S(2)}) async-start(), calls=%async_computation.9 | async-start | bytes 2359296 | tf_op jit(solution)/shard_map/reduce_scatter | solution.py:1526
  377.7 19.0 %collective-permute-start.46 = (bf16[256,2048]{1,0:T(8,128)(2,1)S(1)}, bf16[256,2048]{1,0:T(8,128)(2,1)S(1)}, u32[]{:S(2)}, u32[]{:S(2)}) collective-permute-start(bf16[256,2048]{1,0:T(8,128)(2,1)S(1)} %get-tuple-element.459), channel_id=1, source_target_pairs={{0,8},{8,0},{16,24},{24,16},{1,9},{9,1},{17,25},{25,17},{2,10},{10... | collective-permute-start | bytes 3145736 | tf_op jit(solution)/shard_map/ppermute | solution.py:1444
  378.3 19.8 %collective-permute-start.47 = (bf16[256,2048]{1,0:T(8,128)(2,1)S(1)}, bf16[256,2048]{1,0:T(8,128)(2,1)S(1)}, u32[]{:S(2)}, u32[]{:S(2)}) collective-permute-start(bf16[256,2048]{1,0:T(8,128)(2,1)S(1)} %get-tuple-element.460), channel_id=1, source_target_pairs={{0,16},{8,24},{16,0},{24,8},{1,17},{9,25},{17,1},{25,9},{2,18},{10... | collective-permute-start | bytes 3145736 | tf_op jit(solution)/shard_map/ppermute | solution.py:1444
  401.7 20.6 %collective-permute-start.48 = (bf16[256,2048]{1,0:T(8,128)(2,1)S(1)}, bf16[256,2048]{1,0:T(8,128)(2,1)S(1)}, u32[]{:S(2)}, u32[]{:S(2)}) collective-permute-start(bf16[256,2048]{1,0:T(8,128)(2,1)S(1)} %get-tuple-element.462), channel_id=1, source_target_pairs={{0,8},{8,0},{16,24},{24,16},{1,9},{9,1},{17,25},{25,17},{2,10},{10... | collective-permute-start | bytes 3145736 | tf_op jit(solution)/shard_map/ppermute | solution.py:1401
  402.7 21.3 %collective-permute-start.49 = (bf16[256,2048]{1,0:T(8,128)(2,1)S(1)}, bf16[256,2048]{1,0:T(8,128)(2,1)S(1)}, u32[]{:S(2)}, u32[]{:S(2)}) collective-permute-start(bf16[256,2048]{1,0:T(8,128)(2,1)S(1)} %get-tuple-element.462), channel_id=1, source_target_pairs={{0,16},{8,24},{16,0},{24,8},{1,17},{9,25},{17,1},{25,9},{2,18},{10... | collective-permute-start | bytes 3145736 | tf_op jit(solution)/shard_map/ppermute | solution.py:1402
  449.4 192.6 %reduce-scatter.7.cloned.1.call-start = ((), (), s32[]{:S(2)}) async-start(), calls=%async_computation.8 | async-start | bytes 7077888 | tf_op jit(solution)/shard_map/reduce_scatter | solution.py:1526
  460.6 30.4 %collective-permute-start.54 = (bf16[256,2048]{1,0:T(8,128)(2,1)}, bf16[256,2048]{1,0:T(8,128)(2,1)S(1)}, u32[]{:S(2)}, u32[]{:S(2)}) collective-permute-start(bf16[256,2048]{1,0:T(8,128)(2,1)} %get-tuple-element.466), channel_id=1, source_target_pairs={{0,8},{8,0},{16,24},{24,16},{1,9},{9,1},{17,25},{25,17},{2,10},{10... | collective-permute-start | bytes 3145736 | tf_op jit(solution)/shard_map/ppermute | solution.py:1444
  463.0 28.0 %collective-permute-start.55 = (bf16[256,2048]{1,0:T(8,128)(2,1)}, bf16[256,2048]{1,0:T(8,128)(2,1)S(1)}, u32[]{:S(2)}, u32[]{:S(2)}) collective-permute-start(bf16[256,2048]{1,0:T(8,128)(2,1)} %get-tuple-element.467), channel_id=1, source_target_pairs={{0,16},{8,24},{16,0},{24,8},{1,17},{9,25},{17,1},{25,9},{2,18},{10... | collective-permute-start | bytes 3145736 | tf_op jit(solution)/shard_map/ppermute | solution.py:1444
  493.5 33.0 %collective-permute-start.60 = (bf16[2,128,1408]{2,1,0:T(8,128)(2,1)}, bf16[2,128,1408]{2,1,0:T(8,128)(2,1)}, u32[]{:S(2)}, u32[]{:S(2)}) collective-permute-start(bf16[2,128,1408]{2,1,0:T(8,128)(2,1)} %bitcast.103), channel_id=1, source_target_pairs={{1,3},{2,0},{3,5},{4,2},{5,7},{6,4},{9,11},{10,8},{11,13},{12,10},... | collective-permute-start | bytes 2162696 | tf_op jit(solution)/shard_map/ppermute | solution.py:1530
  538.7 40.3 %collective-permute-start.64 = (bf16[2,128,2816]{2,1,0:T(8,128)(2,1)}, bf16[2,128,2816]{2,1,0:T(8,128)(2,1)}, u32[]{:S(2)}, u32[]{:S(2)}) collective-permute-start(bf16[2,128,2816]{2,1,0:T(8,128)(2,1)} %bitcast.35), channel_id=1, source_target_pairs={{1,3},{2,0},{3,5},{4,2},{5,7},{6,4},{9,11},{10,8},{11,13},{12,10},... | collective-permute-start | bytes 4325384 | tf_op jit(solution)/shard_map/ppermute | solution.py:1530
  552.0 18.4 %collective-permute-start.59 = (bf16[256,2048]{1,0:T(8,128)(2,1)}, bf16[256,2048]{1,0:T(8,128)(2,1)}, u32[]{:S(2)}, u32[]{:S(2)}) collective-permute-start(bf16[256,2048]{1,0:T(8,128)(2,1)} %get-tuple-element.478), channel_id=1, source_target_pairs={{0,16},{8,24},{16,0},{24,8},{1,17},{9,25},{17,1},{25,9},{2,18},{10... | collective-permute-start | bytes 3145736 | tf_op jit(solution)/shard_map/ppermute | solution.py:1444
  579.5 25.3 %collective-permute-start.63 = (bf16[2,128,512]{2,1,0:T(8,128)(2,1)}, bf16[2,128,512]{2,1,0:T(8,128)(2,1)}, u32[]{:S(2)}, u32[]{:S(2)}) collective-permute-start(bf16[2,128,512]{2,1,0:T(8,128)(2,1)} %bitcast.116), channel_id=1, source_target_pairs={{1,3},{2,0},{3,5},{4,2},{5,7},{6,4},{9,11},{10,8},{11,13},{12,10},... | collective-permute-start | bytes 786440 | tf_op jit(solution)/shard_map/ppermute | solution.py:1530
  582.6 43.3 %collective-permute-start.67 = (bf16[2,128,512]{2,1,0:T(8,128)(2,1)}, bf16[2,128,512]{2,1,0:T(8,128)(2,1)S(1)}, u32[]{:S(2)}, u32[]{:S(2)}) collective-permute-start(bf16[2,128,512]{2,1,0:T(8,128)(2,1)} %bitcast.117), channel_id=1, source_target_pairs={{0,1},{1,0},{2,3},{3,2},{4,5},{5,4},{6,7},{7,6},{8,9},{9,8},{10,11... | collective-permute-start | bytes 786440 | tf_op jit(solution)/shard_map/ppermute | solution.py:1461
  585.7 20.8 %collective-permute-start.70 = (f32[8,2048]{1,0:T(8,128)S(1)}, f32[8,2048]{1,0:T(8,128)S(1)}, u32[]{:S(2)}, u32[]{:S(2)}) collective-permute-start(f32[8,2048]{1,0:T(8,128)S(1)} %add.54), channel_id=1, source_target_pairs={{0,16},{8,24},{16,0},{24,8},{1,17},{9,25},{17,1},{25,9},{2,18},{10... | collective-permute-start | bytes 196616 | tf_op jit(solution)/shard_map/ppermute | solution.py:1640
  604.8 21.2 %collective-permute-start.68 = (bf16[2,128,512]{2,1,0:T(8,128)(2,1)}, bf16[2,128,512]{2,1,0:T(8,128)(2,1)S(1)}, u32[]{:S(2)}, u32[]{:S(2)}) collective-permute-start(bf16[2,128,512]{2,1,0:T(8,128)(2,1)} %collective-permute-done.63), channel_id=1, source_target_pairs={{0,1},{1,0},{2,3},{3,2},{4,5},{5,4},{6,7},{7,6},{8,9},{9,8},{10,11... | collective-permute-start | bytes 786440 | tf_op jit(solution)/shard_map/ppermute | solution.py:1461
  (93 other events, 1192.8 us)
Sparse Core Ops, SparseCore 0:
  36.4 86.7 all-gather.3
  133.0 116.7 all-gather.5
  252.0 59.2 all-gather.7
  314.0 82.5 reduce-scatter.4
  398.7 117.6 reduce-scatter.10
  519.1 45.0 reduce-scatter.8
  566.6 75.3 reduce-scatter.6
where the time goes:
time: 687 us; the launch traced here: 678 us
  waiting for transfers between devices  268 us (39%)
  Pallas kernels  169 us (25%)
  matrix products  98.4 us (14%)
  starting transfers between devices  72.1 us (10%)
  local copies, waits for them, and re-layouts  38 us (6%)
  between operations  16.3 us (2%)
  blocking collectives  15.4 us (2%)
    dot_general x10, matrix products, matmul(): lax.dot_general(left, right, (((left_dim,), (right_dim,)), ((), ())), pre...  98.4 us
    ppermute x4, waiting for transfers between devices, share_rows(): by_x = lax.ppermute(own, 'row', x_pairs())  54.3 us
    ppermute x4, waiting for transfers between devices, share_rows(): top = lax.ppermute(by_x[:half], 'row', y_pairs())  42.9 us
    pallas_call x4, Pallas kernels, adam_call(): pl.pallas_call(kernel, grid=grid, in_specs=[smem()] + [state_spec] * 3 +...  35.9 us
    unnamed x142, local copies, waits for them, and re-layouts  33.3 us
    ppermute x4, waiting for transfers between devices, start_home(): return (own, lax.ppermute(own, 'col', outward))  32.3 us
    ppermute x3, waiting for transfers between devices, spread_out(): near = lax.ppermute(sent, 'col', inward)  30.4 us
    ppermute x4, waiting for transfers between devices, scatter_rows(): lax.ppermute(to_x, 'row', x_pairs())  27.3 us
  transfers between devices with their start and end apart: 62, of which 42 were waited for; matrix products, arithmetic and copies ran while one was open for 15% of the time, Pallas kernels for 22%

commit v1 on v0

--- a/solution.py
+++ b/solution.py
@@ -1618,7 +1618,7 @@
     )
     layer_out = finish_out(order, after(middle, mixed_grad), out_partial)
     pulled_one = matmul(after(mixed_grad, layer_out), w_query, 1, 1, BF16)
-    query_sums = matmul(rows_one, after(mixed_grad, pulled_one, down_home[1]), 0, 0, BF16)
+    query_sums = matmul(rows_one, after(mixed_grad, pulled_one, down_own), 0, 0, BF16)
     query_own = sum_up(query_sums)
     gate_home = start_home(after(gate_own, query_sums))
     new_down = adam_flat(

time: 687 us -> 687 us (level)
  waiting for transfers between devices: 268 us -> 253 us
  starting transfers between devices: 72.1 us -> 83.3 us
    ppermute x11, starting transfers between devices: 8.11 us -> 24.6 us  [swap_cores(): lax.ppermute(values, 'col', [(index, index ^ 1) for index in range(column...]
    unnamed x142 -> x140, local copies, waits for them, and re-layouts: 33.3 us -> 33.6 us
  transfers between devices with their start and end apart: 62 -> 62, of which waited for: 42 -> 37; matrix products, arithmetic and copies ran while one was open for 15% -> 16% of each run, Pallas kernels for 22% -> 22%
where the time goes in v1:
time: 687 us; the launch traced here: 678 us
  waiting for transfers between devices  253 us (37%)
  Pallas kernels  170 us (25%)
  matrix products  100 us (15%)
  starting transfers between devices  83.3 us (12%)
  local copies, waits for them, and re-layouts  38.4 us (6%)
  blocking collectives  16.9 us (2%)
  between operations  16.3 us (2%)
    dot_general x10, matrix products, matmul(): lax.dot_general(left, right, (((left_dim,), (right_dim,)), ((), ())), pre...  100 us
    ppermute x4, waiting for transfers between devices, share_rows(): by_x = lax.ppermute(own, 'row', x_pairs())  53.4 us
    ppermute x4, waiting for transfers between devices, share_rows(): top = lax.ppermute(by_x[:half], 'row', y_pairs())  43.5 us
    pallas_call x4, Pallas kernels, adam_call(): pl.pallas_call(kernel, grid=grid, in_specs=[smem()] + [state_spec] * 3 +...  36.7 us
    unnamed x140, local copies, waits for them, and re-layouts  33.6 us
    ppermute x4, waiting for transfers between devices, start_home(): return (own, lax.ppermute(own, 'col', outward))  32.9 us
    ppermute x3, waiting for transfers between devices, spread_out(): near = lax.ppermute(sent, 'col', inward)  32.1 us
    pallas_call x1, Pallas kernels, attend_back(): pl.pallas_call(kernel, grid=(pairs, 3), in_specs=[smem(), smem()] + [colu...  26.7 us
  transfers between devices with their start and end apart: 62, of which 37 were waited for; matrix products, arithmetic and copies ran while one was open for 16% of the time, Pallas kernels for 22%

profile of v1, /device:TPU:0, one launch (start us, length us, event | category | flops | bytes accessed | tf_op | source)
XLA Modules:
  0.0 678.1 jit_solution(17802319057354036243)
XLA Ops:
  21.4 11.0 %collective-permute-done.27 = bf16[2,128,2048]{2,1,0:T(8,128)(2,1)S(1)} collective-permute-done((bf16[2,128,2048]{2,1,0:T(8,128)(2,1)S(1)}, bf16[2,128,2048]{2,1,0:T(8,128)(2,1)S(1)}, u32[]{:S(2)}, u32[]{:S(2)}) %collective-permute-start.27) | collective-permute-done | bytes 1048608 | tf_op jit(solution)/shard_map/ppermute | solution.py:1506
  45.0 17.5 %collective-permute-done.23 = bf16[256,2048]{1,0:T(8,128)(2,1)S(1)} collective-permute-done((bf16[256,2048]{1,0:T(8,128)(2,1)S(1)}, bf16[256,2048]{1,0:T(8,128)(2,1)S(1)}, u32[]{:S(2)}, u32[]{:S(2)}) %collective-permute-start.23) | collective-permute-done | bytes 1048608 | tf_op jit(solution)/shard_map/ppermute | solution.py:1401
  70.3 9.7 %collective-permute-done.25 = bf16[128,2048]{1,0:T(8,128)(2,1)S(1)} collective-permute-done((bf16[128,2048]{1,0:T(8,128)(2,1)S(1)}, bf16[128,2048]{1,0:T(8,128)(2,1)S(1)}, u32[]{:S(2)}, u32[]{:S(2)}) %collective-permute-start.25) | collective-permute-done | bytes 524320 | tf_op jit(solution)/shard_map/ppermute | solution.py:1403
  85.3 16.9 %all_gather.12.in_ref = bf16[32,16,128]{2,1,0:T(8,128)(2,1)S(1)} all-gather(bf16[4,16,128]{2,1,0:T(8,128)(2,1)S(1)} %bitcast_bitcast_fusion), channel_id=1, replica_groups=mesh['row'=4,'col'=8] {'col'}, dimensions={0}, use_global_device_ids=true | all-gather | bytes 147456 | tf_op jit(solution)/shard_map/all_gather | solution.py:1523
  110.4 9.2 %collective-permute-done.31 = bf16[128,2048]{1,0:T(8,128)(2,1)S(1)} collective-permute-done((bf16[128,2048]{1,0:T(8,128)(2,1)S(1)}, bf16[128,2048]{1,0:T(8,128)(2,1)S(1)}, u32[]{:S(2)}, u32[]{:S(2)}) %collective-permute-start.31) | collective-permute-done | bytes 524320 | tf_op jit(solution)/shard_map/ppermute | solution.py:1403
  121.1 9.6 %collective-permute-done.34 = bf16[2,128,2816]{2,1,0:T(8,128)(2,1)S(1)} collective-permute-done((bf16[2,128,2816]{2,1,0:T(8,128)(2,1)S(1)}, bf16[2,128,2816]{2,1,0:T(8,128)(2,1)S(1)}, u32[]{:S(2)}, u32[]{:S(2)}) %collective-permute-start.34) | collective-permute-done | bytes 1441824 | tf_op jit(solution)/shard_map/ppermute | solution.py:1506
  145.9 11.9 %fusion.2.q_ref.k_ref.v_ref = f32[1024,1536]{1,0:T(8,128)} fusion(bf16[1024,2048]{1,0:T(8,128)(2,1)} %copy-done.14, bf16[2048,2048]{1,0:T(8,128)(2,1)} %all-gather.4.cloned.1.call-done), kind=kOutput, calls=%fused_computation.9 | convolution fusion | flops 6442450944 | bytes 16777216 | tf_op jit(solution)/shard_map/dot_general | solution.py:1382
  157.8 11.5 %collective-permute-done.35 = bf16[2,128,1408]{2,1,0:T(8,128)(2,1)} collective-permute-done((bf16[2,128,1408]{2,1,0:T(8,128)(2,1)S(1)}, bf16[2,128,1408]{2,1,0:T(8,128)(2,1)}, u32[]{:S(2)}, u32[]{:S(2)}) %collective-permute-start.35) | collective-permute-done | bytes 720928 | tf_op jit(solution)/shard_map/ppermute | solution.py:1506
  176.3 22.8 %attend.1 = (bf16[1024,512]{1,0:T(8,128)(2,1)S(1)}, bf16[1024,512]{1,0:T(8,128)(2,1)S(1)}, bf16[1024,512]{1,0:T(8,128)(2,1)S(1)}, bf16[1024,512]{1,0:T(8,128)(2,1)S(1)}, f32[4,8,1024]{2,1,0:T(8,128)S(1)}) custom-call(s32[1]{0:T(128)} %bitcast.10.row_ref, s32[1,2]{1,0:T(1,128)S(1)} %copy-done.28, f32[1024,1536]{1,0:T(8,128)S(1)} %copy-done.39, ...), custom_call_target="tpu_custom_call" | custom-call | flops 6442450944 | bytes 10485760 | tf_op jit(solution)/shard_map/attend/pallas_call | solution.py:1075
  218.2 18.4 %collective-permute-done.38.x_ref = bf16[256,2048]{1,0:T(8,128)(2,1)S(1)} collective-permute-done((bf16[256,2048]{1,0:T(8,128)(2,1)S(1)}, bf16[256,2048]{1,0:T(8,128)(2,1)S(1)}, u32[]{:S(2)}, u32[]{:S(2)}) %collective-permute-start.38) | collective-permute-done | bytes 1048608 | tf_op jit(solution)/shard_map/ppermute | solution.py:1444
  242.2 18.4 %collective-permute-done.40 = bf16[256,2048]{1,0:T(8,128)(2,1)S(1)} collective-permute-done((bf16[256,2048]{1,0:T(8,128)(2,1)S(1)}, bf16[256,2048]{1,0:T(8,128)(2,1)S(1)}, u32[]{:S(2)}, u32[]{:S(2)}) %collective-permute-start.40) | collective-permute-done | bytes 1048608 | tf_op jit(solution)/shard_map/ppermute | solution.py:1401
  262.6 12.9 %collective-permute-done.42 = bf16[128,2048]{1,0:T(8,128)(2,1)S(1)} collective-permute-done((bf16[128,2048]{1,0:T(8,128)(2,1)S(1)}, bf16[128,2048]{1,0:T(8,128)(2,1)S(1)}, u32[]{:S(2)}, u32[]{:S(2)}) %collective-permute-start.42) | collective-permute-done | bytes 524320 | tf_op jit(solution)/shard_map/ppermute | solution.py:1403
  281.1 16.7 %gate_up.1 = (bf16[1024,1408]{1,0:T(8,128)(2,1)S(1)}, bf16[1024,1408]{1,0:T(8,128)(2,1)S(1)}, bf16[1024,1408]{1,0:T(8,128)(2,1)S(1)}) custom-call(bf16[1024,2048]{1,0:T(8,128)(2,1)S(1)} %copy-done.21, bf16[2048,2816]{1,0:T(8,128)(2,1)} %all-gather.6.cloned.1.call-done.w_ref), custom_call_target="tpu_custom_call" | custom-call | flops 11811160064 | bytes 24379392 | tf_op jit(solution)/shard_map/gate_up/pallas_call | solution.py:1228
  302.5 8.9 %convolution_convert_fusion.2 = bf16[2048,1408]{1,0:T(8,128)(2,1)} fusion(bf16[1024,2048]{1,0:T(8,128)(2,1)S(1)} %copy-done.18, bf16[1024,1408]{1,0:T(8,128)(2,1)S(1)} %get-tuple-element.458), kind=kOutput, calls=%fused_computation.6 | convolution fusion | flops 5908463616 | bytes 12845056 | tf_op jit(solution)/shard_map/dot_general | solution.py:1382
  317.4 12.2 %gate_up_back.1 = bf16[1024,2816]{1,0:T(8,128)(2,1)} custom-call(bf16[1024,2048]{1,0:T(8,128)(2,1)S(1)} %copy-done.19, bf16[2048,1408]{1,0:T(8,128)(2,1)} %all-gather.8.cloned.1.call-done.w_ref, bf16[1024,1408]{1,0:T(8,128)(2,1)S(1)} %copy-done.36, bf16[1024,1408]{1,0:T(8,128)(2,1)S(1)} %copy-done.38), custom_call_target="tpu_custom_call" | custom-call | flops 5905580032 | bytes 21495808 | tf_op jit(solution)/shard_map/gate_up_back/pallas_call | solution.py:1263
  329.6 18.1 %convolution_convert_fusion.3.one_ref.two_ref.own_ref = bf16[1024,2048]{1,0:T(8,128)(2,1)} fusion(bf16[1024,2816]{1,0:T(8,128)(2,1)} %gate_up_back.1, bf16[2048,2816]{1,0:T(8,128)(2,1)} %all-gather.6.cloned.1.call-done.w_ref), kind=kOutput, calls=%fused_computation.11 | convolution fusion | flops 11813257216 | bytes 21495808 | tf_op jit(solution)/shard_map/dot_general | solution.py:1382
  347.7 15.1 %convolution_convert_fusion = bf16[2048,2816]{1,0:T(8,128)(2,1)} fusion(bf16[1024,2048]{1,0:T(8,128)(2,1)S(1)} %copy-done.22, bf16[1024,2816]{1,0:T(8,128)(2,1)S(1)} %copy-done.62), kind=kOutput, calls=%fused_computation.4 | convolution fusion | flops 11816927232 | bytes 21495808 | tf_op jit(solution)/shard_map/dot_general | solution.py:1382
  367.0 6.5 collective-permute-done.45.bottom_ref
  379.8 9.4 %convolution_convert_fusion.4.one_ref.two_ref.own_ref = bf16[1024,2048]{1,0:T(8,128)(2,1)S(1)} fusion(bf16[1024,1408]{1,0:T(8,128)(2,1)S(1)} %copy-done.50, bf16[2048,1408]{1,0:T(8,128)(2,1)} %all-gather.8.cloned.1.call-done.w_ref), kind=kOutput, calls=%fused_computation.13 | convolution fusion | flops 5907677184 | bytes 12845056 | tf_op jit(solution)/shard_map/dot_general | solution.py:1382
  389.2 7.6 %collective-permute-done.46.x_ref = bf16[256,2048]{1,0:T(8,128)(2,1)S(1)} collective-permute-done((bf16[256,2048]{1,0:T(8,128)(2,1)S(1)}, bf16[256,2048]{1,0:T(8,128)(2,1)S(1)}, u32[]{:S(2)}, u32[]{:S(2)}) %collective-permute-start.46) | collective-permute-done | bytes 1048608 | tf_op jit(solution)/shard_map/ppermute | solution.py:1444
  403.6 17.6 %collective-permute-done.48 = bf16[256,2048]{1,0:T(8,128)(2,1)S(1)} collective-permute-done((bf16[256,2048]{1,0:T(8,128)(2,1)S(1)}, bf16[256,2048]{1,0:T(8,128)(2,1)S(1)}, u32[]{:S(2)}, u32[]{:S(2)}) %collective-permute-start.48) | collective-permute-done | bytes 1048608 | tf_op jit(solution)/shard_map/ppermute | solution.py:1401
  423.8 11.7 %collective-permute-done.50 = bf16[128,2048]{1,0:T(8,128)(2,1)S(1)} collective-permute-done((bf16[128,2048]{1,0:T(8,128)(2,1)S(1)}, bf16[128,2048]{1,0:T(8,128)(2,1)S(1)}, u32[]{:S(2)}, u32[]{:S(2)}) %collective-permute-start.50) | collective-permute-done | bytes 524320 | tf_op jit(solution)/shard_map/ppermute | solution.py:1403
  458.1 26.7 %attend_back.1 = (bf16[1024,1536]{1,0:T(8,128)(2,1)}, f32[8,1536]{1,0:T(8,128)S(1)}) custom-call(s32[1]{0:T(128)} %bitcast.10.row_ref, s32[1,2]{1,0:T(1,128)S(1)} %copy-done.28, bf16[1024,512]{1,0:T(8,128)(2,1)S(1)} %copy-done.44, bf16[1024,512]{1,0:T(8,128)(2,1)S(1)} %copy-done.46, bf16[1024,512]{1,0:T(8,128)(2,1)S(1)} %copy-done.48, ...), custom_call_target="tpu_custom_call" | custom-call | flops 17179869184 | bytes 10485760 | tf_op jit(solution)/shard_map/attend_back/pallas_call | solution.py:1184
  487.5 11.0 %fusion.4.one_ref.two_ref.own_ref = bf16[1024,2048]{1,0:T(8,128)(2,1)} fusion(bf16[1024,1536]{1,0:T(8,128)(2,1)S(1)} %copy-done.63, bf16[2048,2048]{1,0:T(8,128)(2,1)} %all-gather.4.cloned.1.call-done), kind=kOutput, calls=%fused_computation.12 | convolution fusion | flops 6444548096 | bytes 13631488 | tf_op jit(solution)/shard_map/dot_general | solution.py:1382
  498.5 11.9 %convolution_convert_fusion.1 = bf16[2048,1536]{1,0:T(8,128)(2,1)} fusion(bf16[1024,2048]{1,0:T(8,128)(2,1)} %copy-done.14, bf16[1024,1536]{1,0:T(8,128)(2,1)} %get-tuple-element.479), kind=kOutput, calls=%fused_computation.5 | convolution fusion | flops 6445596672 | bytes 13631488 | tf_op jit(solution)/shard_map/dot_general | solution.py:1382
  529.8 14.7 %collective-permute-start.61 = (bf16[2,128,1408]{2,1,0:T(8,128)(2,1)S(1)}, bf16[2,128,1408]{2,1,0:T(8,128)(2,1)S(1)}, u32[]{:S(2)}, u32[]{:S(2)}) collective-permute-start(bf16[2,128,1408]{2,1,0:T(8,128)(2,1)S(1)} %bitcast.104), channel_id=1, source_target_pairs={{0,1},{1,0},{2,3},{3,2},{4,5},{5,4},{6,7},{7,6},{8,9},{9,8},{10,11... | collective-permute-start | bytes 2162696 | tf_op jit(solution)/shard_map/ppermute | solution.py:1461
  544.5 15.7 %collective-permute-done.60 = bf16[2,128,1408]{2,1,0:T(8,128)(2,1)} collective-permute-done((bf16[2,128,1408]{2,1,0:T(8,128)(2,1)S(1)}, bf16[2,128,1408]{2,1,0:T(8,128)(2,1)}, u32[]{:S(2)}, u32[]{:S(2)}) %collective-permute-start.60) | collective-permute-done | bytes 720928 | tf_op jit(solution)/shard_map/ppermute | solution.py:1530
  565.2 9.2 %adam_down.1 = (f32[512,1408]{1,0:T(8,128)}, f32[512,1408]{1,0:T(8,128)}, f32[512,1408]{1,0:T(8,128)}) custom-call(s32[32]{0:T(128)} %copy-done.61, f32[512,1408]{1,0:T(8,128)} %m_ref.2, f32[512,1408]{1,0:T(8,128)} %f_ref.2, f32[512,1408]{1,0:T(8,128)} %s_ref.2, bf16[4,128,1408]{2,1,0:T(8,128)(2,1)} %get-tuple-element.519.g_ref), custom_call_target="tpu_custom_call" | custom-call | flops 8650752 | bytes 18743296 | tf_op jit(solution)/shard_map/adam_down/pallas_call | solution.py:1311
  601.4 13.9 %adam_gate.1 = (f32[11264,128]{1,0:T(8,128)}, f32[11264,128]{1,0:T(8,128)}, f32[11264,128]{1,0:T(8,128)}) custom-call(s32[32]{0:T(128)} %copy-done.61, f32[11264,128]{1,0:T(8,128)} %bitcast.95, f32[11264,128]{1,0:T(8,128)} %bitcast.111, f32[11264,128]{1,0:T(8,128)} %bitcast.112, bf16[4,128,2816]{2,1,0:T(8,128)(2,1)} %get-tuple-element.520.g_ref), custom_call_target="tpu_custom_call" | custom-call | flops 17301504 | bytes 37486592 | tf_op jit(solution)/shard_map/adam_gate/pallas_call | solution.py:1311
  625.9 8.3 %collective-permute-done.73 = f32[8,2048]{1,0:T(8,128)S(1)} collective-permute-done((f32[8,2048]{1,0:T(8,128)S(1)}, f32[8,2048]{1,0:T(8,128)S(1)}, u32[]{:S(2)}, u32[]{:S(2)}) %collective-permute-start.73) | collective-permute-done | bytes 65568 | tf_op jit(solution)/shard_map/ppermute | solution.py:1640
  644.6 11.6 %collective-permute-done.74 = bf16[2,128,1536]{2,1,0:T(8,128)(2,1)S(1)} collective-permute-done((bf16[2,128,1536]{2,1,0:T(8,128)(2,1)}, bf16[2,128,1536]{2,1,0:T(8,128)(2,1)S(1)}, u32[]{:S(2)}, u32[]{:S(2)}) %collective-permute-start.74) | collective-permute-done | bytes 786464 | tf_op jit(solution)/shard_map/ppermute | solution.py:1530
  661.7 9.1 %adam_query.1 = (f32[3,512,512]{2,1,0:T(8,128)}, f32[3,512,512]{2,1,0:T(8,128)}, f32[3,512,512]{2,1,0:T(8,128)}) custom-call(s32[32]{0:T(128)} %copy-done.61, f32[3,512,512]{2,1,0:T(8,128)} %bitcast.97, f32[3,512,512]{2,1,0:T(8,128)} %bitcast.121, f32[3,512,512]{2,1,0:T(8,128)} %bitcast.122, bf16[4,128,1536]{2,1,0:T(8,128)(2,1)} %get-tuple-element.522.g_ref), custom_call_target="tpu_custom_call" | custom-call | flops 9437184 | bytes 20447232 | tf_op jit(solution)/shard_map/adam_query/pallas_call | solution.py:1311
  (318 shorter events, 254.4 us)
Async XLA Ops:
  7.2 138.7 %all-gather.4.cloned.1.call-start = ((), (), s32[]{:S(2)}) async-start(), calls=%async_computation.4 | async-start | bytes 9437184 | tf_op jit(solution)/shard_map/all_gather | solution.py:1523
  35.3 243.6 %all-gather.6.cloned.1.call-start = ((), (), s32[]{:S(2)}) async-start(), calls=%async_computation.5 | async-start | bytes 12976128 | tf_op jit(solution)/shard_map/all_gather | solution.py:1523
  36.7 25.7 %collective-permute-start.23 = (bf16[256,2048]{1,0:T(8,128)(2,1)S(1)}, bf16[256,2048]{1,0:T(8,128)(2,1)S(1)}, u32[]{:S(2)}, u32[]{:S(2)}) collective-permute-start(bf16[256,2048]{1,0:T(8,128)(2,1)S(1)} %norm_one.1), channel_id=1, source_target_pairs={{0,8},{8,0},{16,24},{24,16},{1,9},{9,1},{17,25},{25,17},{2,10},{10... | collective-permute-start | bytes 3145736 | tf_op jit(solution)/shard_map/ppermute | solution.py:1401
  43.1 59.6 %collective-permute-start.33 = (bf16[4,128,2816]{2,1,0:T(8,128)(2,1)}, bf16[4,128,2816]{2,1,0:T(8,128)(2,1)S(1)}, u32[]{:S(2)}, u32[]{:S(2)}) collective-permute-start(bf16[4,128,2816]{2,1,0:T(8,128)(2,1)} %pack_gate.1.refs_0_), channel_id=1, source_target_pairs={{0,1},{1,0},{2,3},{3,2},{4,5},{5,4},{6,7},{7,6},{8,9},{9,8},{10,11... | collective-permute-start | bytes 8650760 | tf_op jit(solution)/shard_map/ppermute | solution.py:1461
  43.4 26.0 %collective-permute-start.24 = (bf16[256,2048]{1,0:T(8,128)(2,1)S(1)}, bf16[256,2048]{1,0:T(8,128)(2,1)S(1)}, u32[]{:S(2)}, u32[]{:S(2)}) collective-permute-start(bf16[256,2048]{1,0:T(8,128)(2,1)S(1)} %norm_one.1), channel_id=1, source_target_pairs={{0,16},{8,24},{16,0},{24,8},{1,17},{9,25},{17,1},{25,9},{2,18},{10... | collective-permute-start | bytes 3145736 | tf_op jit(solution)/shard_map/ppermute | solution.py:1402
  83.1 23.2 %collective-permute-start.29 = (bf16[256,2048]{1,0:T(8,128)(2,1)S(1)}, bf16[256,2048]{1,0:T(8,128)(2,1)S(1)}, u32[]{:S(2)}, u32[]{:S(2)}) collective-permute-start(bf16[256,2048]{1,0:T(8,128)(2,1)S(1)} %order_grad.1), channel_id=1, source_target_pairs={{0,8},{8,0},{16,24},{24,16},{1,9},{9,1},{17,25},{25,17},{2,10},{10... | collective-permute-start | bytes 3145736 | tf_op jit(solution)/shard_map/ppermute | solution.py:1401
  83.7 25.3 %collective-permute-start.30 = (bf16[256,2048]{1,0:T(8,128)(2,1)S(1)}, bf16[256,2048]{1,0:T(8,128)(2,1)S(1)}, u32[]{:S(2)}, u32[]{:S(2)}) collective-permute-start(bf16[256,2048]{1,0:T(8,128)(2,1)S(1)} %order_grad.1), channel_id=1, source_target_pairs={{0,16},{8,24},{16,0},{24,8},{1,17},{9,25},{17,1},{25,9},{2,18},{10... | collective-permute-start | bytes 3145736 | tf_op jit(solution)/shard_map/ppermute | solution.py:1402
  104.0 26.7 %collective-permute-start.34 = (bf16[2,128,2816]{2,1,0:T(8,128)(2,1)S(1)}, bf16[2,128,2816]{2,1,0:T(8,128)(2,1)S(1)}, u32[]{:S(2)}, u32[]{:S(2)}) collective-permute-start(bf16[2,128,2816]{2,1,0:T(8,128)(2,1)S(1)} %pick_blocks.58), channel_id=1, source_target_pairs={{0,2},{2,4},{3,1},{4,6},{5,3},{7,5},{8,10},{10,12},{11,9},{12,14},... | collective-permute-start | bytes 4325384 | tf_op jit(solution)/shard_map/ppermute | solution.py:1506
  133.0 178.6 %all-gather.8.cloned.1.call-start = ((), (), s32[]{:S(2)}) async-start(), calls=%async_computation.6 | async-start | bytes 6488064 | tf_op jit(solution)/shard_map/all_gather | solution.py:1523
  140.7 28.6 %collective-permute-start.35 = (bf16[2,128,1408]{2,1,0:T(8,128)(2,1)S(1)}, bf16[2,128,1408]{2,1,0:T(8,128)(2,1)}, u32[]{:S(2)}, u32[]{:S(2)}) collective-permute-start(bf16[2,128,1408]{2,1,0:T(8,128)(2,1)S(1)} %pick_blocks.59), channel_id=1, source_target_pairs={{0,2},{2,4},{3,1},{4,6},{5,3},{7,5},{8,10},{10,12},{11,9},{12,14},... | collective-permute-start | bytes 2162696 | tf_op jit(solution)/shard_map/ppermute | solution.py:1506
  171.1 327.4 %reduce-scatter.5.cloned.1.call-start = ((), (), s32[]{:S(2)}) async-start(), calls=%async_computation.7 | async-start | bytes 6488064 | tf_op jit(solution)/shard_map/reduce_scatter | solution.py:1526
  216.1 20.5 %collective-permute-start.38 = (bf16[256,2048]{1,0:T(8,128)(2,1)S(1)}, bf16[256,2048]{1,0:T(8,128)(2,1)S(1)}, u32[]{:S(2)}, u32[]{:S(2)}) collective-permute-start(bf16[256,2048]{1,0:T(8,128)(2,1)S(1)} %get-tuple-element.449), channel_id=1, source_target_pairs={{0,8},{8,0},{16,24},{24,16},{1,9},{9,1},{17,25},{25,17},{2,10},{10... | collective-permute-start | bytes 3145736 | tf_op jit(solution)/shard_map/ppermute | solution.py:1444
  216.8 20.4 %collective-permute-start.39 = (bf16[256,2048]{1,0:T(8,128)(2,1)S(1)}, bf16[256,2048]{1,0:T(8,128)(2,1)S(1)}, u32[]{:S(2)}, u32[]{:S(2)}) collective-permute-start(bf16[256,2048]{1,0:T(8,128)(2,1)S(1)} %get-tuple-element.450), channel_id=1, source_target_pairs={{0,16},{8,24},{16,0},{24,8},{1,17},{9,25},{17,1},{25,9},{2,18},{10... | collective-permute-start | bytes 3145736 | tf_op jit(solution)/shard_map/ppermute | solution.py:1444
  239.3 21.3 %collective-permute-start.40 = (bf16[256,2048]{1,0:T(8,128)(2,1)S(1)}, bf16[256,2048]{1,0:T(8,128)(2,1)S(1)}, u32[]{:S(2)}, u32[]{:S(2)}) collective-permute-start(bf16[256,2048]{1,0:T(8,128)(2,1)S(1)} %get-tuple-element.452), channel_id=1, source_target_pairs={{0,8},{8,0},{16,24},{24,16},{1,9},{9,1},{17,25},{25,17},{2,10},{10... | collective-permute-start | bytes 3145736 | tf_op jit(solution)/shard_map/ppermute | solution.py:1401
  240.7 21.5 %collective-permute-start.41 = (bf16[256,2048]{1,0:T(8,128)(2,1)S(1)}, bf16[256,2048]{1,0:T(8,128)(2,1)S(1)}, u32[]{:S(2)}, u32[]{:S(2)}) collective-permute-start(bf16[256,2048]{1,0:T(8,128)(2,1)S(1)} %get-tuple-element.452), channel_id=1, source_target_pairs={{0,16},{8,24},{16,0},{24,8},{1,17},{9,25},{17,1},{25,9},{2,18},{10... | collective-permute-start | bytes 3145736 | tf_op jit(solution)/shard_map/ppermute | solution.py:1402
  311.5 207.0 %reduce-scatter.11.cloned.1.call-start = ((), (), s32[]{:S(2)}) async-start(), calls=%async_computation.10 | async-start | bytes 12976128 | tf_op jit(solution)/shard_map/reduce_scatter | solution.py:1526
  362.9 225.7 %reduce-scatter.9.cloned.1.call-start = ((), (), s32[]{:S(2)}) async-start(), calls=%async_computation.9 | async-start | bytes 2359296 | tf_op jit(solution)/shard_map/reduce_scatter | solution.py:1526
  378.6 19.8 %collective-permute-start.47 = (bf16[256,2048]{1,0:T(8,128)(2,1)S(1)}, bf16[256,2048]{1,0:T(8,128)(2,1)S(1)}, u32[]{:S(2)}, u32[]{:S(2)}) collective-permute-start(bf16[256,2048]{1,0:T(8,128)(2,1)S(1)} %get-tuple-element.460), channel_id=1, source_target_pairs={{0,16},{8,24},{16,0},{24,8},{1,17},{9,25},{17,1},{25,9},{2,18},{10... | collective-permute-start | bytes 3145736 | tf_op jit(solution)/shard_map/ppermute | solution.py:1444
  402.1 19.1 %collective-permute-start.48 = (bf16[256,2048]{1,0:T(8,128)(2,1)S(1)}, bf16[256,2048]{1,0:T(8,128)(2,1)S(1)}, u32[]{:S(2)}, u32[]{:S(2)}) collective-permute-start(bf16[256,2048]{1,0:T(8,128)(2,1)S(1)} %get-tuple-element.462), channel_id=1, source_target_pairs={{0,8},{8,0},{16,24},{24,16},{1,9},{9,1},{17,25},{25,17},{2,10},{10... | collective-permute-start | bytes 3145736 | tf_op jit(solution)/shard_map/ppermute | solution.py:1401
  402.4 20.4 %collective-permute-start.49 = (bf16[256,2048]{1,0:T(8,128)(2,1)S(1)}, bf16[256,2048]{1,0:T(8,128)(2,1)S(1)}, u32[]{:S(2)}, u32[]{:S(2)}) collective-permute-start(bf16[256,2048]{1,0:T(8,128)(2,1)S(1)} %get-tuple-element.462), channel_id=1, source_target_pairs={{0,16},{8,24},{16,0},{24,8},{1,17},{9,25},{17,1},{25,9},{2,18},{10... | collective-permute-start | bytes 3145736 | tf_op jit(solution)/shard_map/ppermute | solution.py:1402
  447.7 194.4 %reduce-scatter.7.cloned.1.call-start = ((), (), s32[]{:S(2)}) async-start(), calls=%async_computation.8 | async-start | bytes 7077888 | tf_op jit(solution)/shard_map/reduce_scatter | solution.py:1526
  456.4 28.5 %collective-permute-start.54 = (bf16[256,2048]{1,0:T(8,128)(2,1)}, bf16[256,2048]{1,0:T(8,128)(2,1)S(1)}, u32[]{:S(2)}, u32[]{:S(2)}) collective-permute-start(bf16[256,2048]{1,0:T(8,128)(2,1)} %get-tuple-element.466), channel_id=1, source_target_pairs={{0,8},{8,0},{16,24},{24,16},{1,9},{9,1},{17,25},{25,17},{2,10},{10... | collective-permute-start | bytes 3145736 | tf_op jit(solution)/shard_map/ppermute | solution.py:1444
  457.7 27.2 %collective-permute-start.55 = (bf16[256,2048]{1,0:T(8,128)(2,1)}, bf16[256,2048]{1,0:T(8,128)(2,1)S(1)}, u32[]{:S(2)}, u32[]{:S(2)}) collective-permute-start(bf16[256,2048]{1,0:T(8,128)(2,1)} %get-tuple-element.467), channel_id=1, source_target_pairs={{0,16},{8,24},{16,0},{24,8},{1,17},{9,25},{17,1},{25,9},{2,18},{10... | collective-permute-start | bytes 3145736 | tf_op jit(solution)/shard_map/ppermute | solution.py:1444
  514.4 45.8 %collective-permute-start.60 = (bf16[2,128,1408]{2,1,0:T(8,128)(2,1)S(1)}, bf16[2,128,1408]{2,1,0:T(8,128)(2,1)}, u32[]{:S(2)}, u32[]{:S(2)}) collective-permute-start(bf16[2,128,1408]{2,1,0:T(8,128)(2,1)S(1)} %bitcast.103), channel_id=1, source_target_pairs={{1,3},{2,0},{3,5},{4,2},{5,7},{6,4},{9,11},{10,8},{11,13},{12,10},... | collective-permute-start | bytes 2162696 | tf_op jit(solution)/shard_map/ppermute | solution.py:1530
  518.4 70.1 %collective-permute-start.64 = (bf16[2,128,2816]{2,1,0:T(8,128)(2,1)}, bf16[2,128,2816]{2,1,0:T(8,128)(2,1)}, u32[]{:S(2)}, u32[]{:S(2)}) collective-permute-start(bf16[2,128,2816]{2,1,0:T(8,128)(2,1)} %bitcast.35), channel_id=1, source_target_pairs={{1,3},{2,0},{3,5},{4,2},{5,7},{6,4},{9,11},{10,8},{11,13},{12,10},... | collective-permute-start | bytes 4325384 | tf_op jit(solution)/shard_map/ppermute | solution.py:1530
  527.5 46.9 %collective-permute-start.58 = (bf16[256,2048]{1,0:T(8,128)(2,1)}, bf16[256,2048]{1,0:T(8,128)(2,1)S(1)}, u32[]{:S(2)}, u32[]{:S(2)}) collective-permute-start(bf16[256,2048]{1,0:T(8,128)(2,1)} %get-tuple-element.477), channel_id=1, source_target_pairs={{0,8},{8,0},{16,24},{24,16},{1,9},{9,1},{17,25},{25,17},{2,10},{10... | collective-permute-start | bytes 3145736 | tf_op jit(solution)/shard_map/ppermute | solution.py:1444
  527.7 46.7 %collective-permute-start.59 = (bf16[256,2048]{1,0:T(8,128)(2,1)}, bf16[256,2048]{1,0:T(8,128)(2,1)}, u32[]{:S(2)}, u32[]{:S(2)}) collective-permute-start(bf16[256,2048]{1,0:T(8,128)(2,1)} %get-tuple-element.478), channel_id=1, source_target_pairs={{0,16},{8,24},{16,0},{24,8},{1,17},{9,25},{17,1},{25,9},{2,18},{10... | collective-permute-start | bytes 3145736 | tf_op jit(solution)/shard_map/ppermute | solution.py:1444
  529.8 30.4 %collective-permute-start.61 = (bf16[2,128,1408]{2,1,0:T(8,128)(2,1)S(1)}, bf16[2,128,1408]{2,1,0:T(8,128)(2,1)S(1)}, u32[]{:S(2)}, u32[]{:S(2)}) collective-permute-start(bf16[2,128,1408]{2,1,0:T(8,128)(2,1)S(1)} %bitcast.104), channel_id=1, source_target_pairs={{0,1},{1,0},{2,3},{3,2},{4,5},{5,4},{6,7},{7,6},{8,9},{9,8},{10,11... | collective-permute-start | bytes 2162696 | tf_op jit(solution)/shard_map/ppermute | solution.py:1461
  588.5 26.8 %collective-permute-start.63 = (bf16[2,128,512]{2,1,0:T(8,128)(2,1)}, bf16[2,128,512]{2,1,0:T(8,128)(2,1)}, u32[]{:S(2)}, u32[]{:S(2)}) collective-permute-start(bf16[2,128,512]{2,1,0:T(8,128)(2,1)} %bitcast.116), channel_id=1, source_target_pairs={{1,3},{2,0},{3,5},{4,2},{5,7},{6,4},{9,11},{10,8},{11,13},{12,10},... | collective-permute-start | bytes 786440 | tf_op jit(solution)/shard_map/ppermute | solution.py:1530
  591.1 44.5 %collective-permute-start.67 = (bf16[2,128,512]{2,1,0:T(8,128)(2,1)}, bf16[2,128,512]{2,1,0:T(8,128)(2,1)S(1)}, u32[]{:S(2)}, u32[]{:S(2)}) collective-permute-start(bf16[2,128,512]{2,1,0:T(8,128)(2,1)} %bitcast.117), channel_id=1, source_target_pairs={{0,1},{1,0},{2,3},{3,2},{4,5},{5,4},{6,7},{7,6},{8,9},{9,8},{10,11... | collective-permute-start | bytes 786440 | tf_op jit(solution)/shard_map/ppermute | solution.py:1461
  595.3 21.9 %collective-permute-start.70 = (f32[8,2048]{1,0:T(8,128)S(1)}, f32[8,2048]{1,0:T(8,128)S(1)}, u32[]{:S(2)}, u32[]{:S(2)}) collective-permute-start(f32[8,2048]{1,0:T(8,128)S(1)} %add.54), channel_id=1, source_target_pairs={{0,16},{8,24},{16,0},{24,8},{1,17},{9,25},{17,1},{25,9},{2,18},{10... | collective-permute-start | bytes 196616 | tf_op jit(solution)/shard_map/ppermute | solution.py:1640
  615.3 20.2 %collective-permute-start.68 = (bf16[2,128,512]{2,1,0:T(8,128)(2,1)}, bf16[2,128,512]{2,1,0:T(8,128)(2,1)S(1)}, u32[]{:S(2)}, u32[]{:S(2)}) collective-permute-start(bf16[2,128,512]{2,1,0:T(8,128)(2,1)} %collective-permute-done.63), channel_id=1, source_target_pairs={{0,1},{1,0},{2,3},{3,2},{4,5},{5,4},{6,7},{7,6},{8,9},{9,8},{10,11... | collective-permute-start | bytes 786440 | tf_op jit(solution)/shard_map/ppermute | solution.py:1461
  (92 other events, 1125.8 us)
Sparse Core Ops, SparseCore 0:
  35.4 87.7 all-gather.3
  133.1 116.7 all-gather.5
  252.1 59.2 all-gather.7
  314.1 84.4 reduce-scatter.4
  400.7 117.6 reduce-scatter.10
  521.2 36.7 reduce-scatter.8
  560.3 81.7 reduce-scatter.6
